TPU v7x, 32 devices: a whole 2x2x4 slice. The times are simulated.
32 devices in a mesh: dp: 4 (over y, x), ctx: 8 (over z, core).
Axes of the slice: x: 2, y: 2, z: 4, core: 2. Of those that a mesh axis runs over, the one named last changes fastest.
Arguments:
- inputs: bfloat16 [8192, 8192], P(('dp', 'ctx')), parts along dimension 0, may hold values from -6 to 6
- key_query: bfloat16 [8192, 2048], P(('dp', 'ctx')), parts along dimension 0, may hold values from -3 to 3
- conv_inputs: float32 [4, 8192], replicated, may hold values from -3 to 3
- conv_kq: float32 [4, 2048], replicated, may hold values from -3 to 3
- step_size: float32 [8192, 128], P(('dp', 'ctx')), parts along dimension 0, may hold values from 0.1 to 1
- decay_log: float32 [8192, 128], P(('dp', 'ctx')), parts along dimension 0, may hold values from -1 to 0, as said below
- skip_gain: float32 [128], replicated, may hold values from 0.5 to 1.5
- norm_gain: float32 [8192], replicated, may hold values from 0.5 to 1.5
Outputs:
- mixed: bfloat16 [8192, 8192], P('dp', 'ctx'), parts along dimension 0
There are 4 independent parts, one for each index of `dp`. A program takes and returns all parts, laid end to end along the dimension named above; an argument that names none is the same for every part. Nothing has to cross between parts.
Inputs may be any that keep to these rules, and one draw needn't show every extreme that they name: `decay_log`: log decay factors, all negative.
All inputs are finite; a program needn't handle non-finite values.
Results may differ from a plain program's by a relative error of at most 0.0085.
Values may be sent and summed in bfloat16 or wider, within the bound.
No kernel may reach another device: no remote copies, remote signals or barrier semaphores. Data moves between devices by JAX's collectives and lax.ppermute only.
A program may use at most 448 MiB of HBM per device.

v0:
```python
import functools

import jax
import jax.numpy as jnp
from jax import lax
from jax.experimental import pallas as pl
from jax.experimental.pallas import tpu as pltpu
from jax.sharding import PartitionSpec as P

HEADS = 128
HEAD_DIM = 64
STATE = 128
GROUPS = 8
KW = 4
BLOCK = 128
GROUP_WIDTH = HEADS * HEAD_DIM // GROUPS
EPS = 1e-05
HALO = 16
LANES = 128
SUBLANES = 8
FIELDS = 2
STRIP = 64
PAIR = 2
WINDOW = 3
ORDER = (4, 1, 7, 3, 2, 5, 6)
PACK_VMEM = 58 * 1024 * 1024
VMEM_LIMIT = 28 * 1024 * 1024


def contract(a, b, dims):
    return lax.dot_general(a, b, (dims, ((), ())), preferred_element_type=jnp.float32)


def as_parts(v, count):
    parts = []
    for _ in range(count):
        part = v.astype(jnp.bfloat16)
        parts.append(part)
        v = v - part.astype(jnp.float32)
    return parts


def scalar_units(heads, rows, cols):
    units = []
    for p in range(FIELDS):
        for head in range(0, heads, SUBLANES):
            line, column = divmod(len(units), cols // rows)
            units.append((p, head, min(SUBLANES, heads), line * SUBLANES, column * rows))
    return units


def pack_kernel(peers, span, width, heads, codes, *refs):
    owner_ref, x_ref, kq_ref, decay_ref, step_ref = refs[:5]
    outs = refs[5 : 5 + len(codes)]
    raw_scalars, scalars, kq_near, sems = refs[5 + len(codes) :]
    rows = x_ref.shape[0]
    copies = [
        pltpu.make_async_copy(ref, dst, sems.at[1, i])
        for i, (ref, dst) in enumerate(
            ((decay_ref, raw_scalars.at[0]), (step_ref, raw_scalars.at[1]), (kq_ref, kq_near))
        )
    ]
    owners = [owner_ref[code] for code in codes]
    for i, owner in enumerate(owners):
        column = pl.multiple_of(owner * width, LANES)
        copies.append(
            pltpu.make_async_copy(
                x_ref.at[:, pl.ds(column, width)], outs[i].at[0:rows, 0:width], sems.at[0, i]
            )
        )
    for copy in copies:
        copy.start()
    for copy in copies[:3]:
        copy.wait()
    for p in range(FIELDS):
        field = raw_scalars[p].T
        for owner in range(peers):
            scalars[p, owner] = field[owner * heads : (owner + 1) * heads]
    for i, owner in enumerate(owners):
        outs[i][rows:] = jnp.zeros((outs[i].shape[0] - rows, outs[i].shape[1]), jnp.bfloat16)
        for p, head, count, top, left in scalar_units(heads, rows, width + 2 * STATE):
            outs[i][rows + top : rows + top + count, left : left + rows] = scalars[
                p, owner, head : head + count
            ].astype(jnp.bfloat16)
        for j in range(2):
            column = pl.multiple_of((j * GROUPS + owner // span) * STATE, LANES)
            left = width + j * STATE
            outs[i][0:rows, left : left + STATE] = kq_near[:, pl.ds(column, STATE)]
    for copy in copies[3:]:
        copy.wait()


def spread(heads):
    head_of = lax.broadcasted_iota(jnp.int32, (2 * heads, heads * HEAD_DIM), 1) // HEAD_DIM
    row = lax.rem(lax.broadcasted_iota(jnp.int32, (2 * heads, heads * HEAD_DIM), 0), heads)
    return jnp.where(head_of == row, 1.0, 0.0).astype(jnp.bfloat16)


def local_kernel(width, heads, count, chained, *refs):
    source_ref = refs[0]
    parts = refs[1 : 1 + 2 * count]
    taps_ref, skip_ref = refs[1 + 2 * count : 3 + 2 * count]
    refs = refs[3 + 2 * count + (4 if chained else 0) :]
    pre, state, c_out, outward_out = refs[:4]
    wide, x_ref, scaled_ref, scales = refs[4:]
    rows = x_ref.shape[0]
    blocks = rows // BLOCK
    full = width + 2 * STATE
    row = lax.broadcasted_iota(jnp.int32, (rows, rows), 0)
    col = lax.broadcasted_iota(jnp.int32, (rows, rows), 1)
    lower = (row >= col) & (row // BLOCK == col // BLOCK)
    ones = jnp.where(lower, 1.0, 0.0).astype(jnp.bfloat16)
    eye = jnp.where(row == col, 1.0, 0.0).astype(jnp.bfloat16)
    expand = spread(heads)

    for which in range(count):
        source = source_ref[which]
        part, earlier = parts[2 * which : 2 * which + 2]
        wide[HALO:] = part[0:rows, 0:full]
        edge = earlier[rows - HALO : rows, 0:full]
        wide[0:HALO] = jnp.where(source == 0, jnp.zeros_like(edge), edge)

        def activated(r, lane):
            tap = [taps_ref[k : k + 1, lane : lane + LANES] for k in range(KW)]
            now = wide[r : r + STRIP + HALO, lane : lane + LANES].astype(jnp.float32)
            now = now[HALO // 2 :]
            before = pltpu.roll(now, 1, 0)
            older = pltpu.roll(tap[0] * before + tap[1] * now, 2, 0)
            summed = (older + (tap[2] * before + tap[3] * now))[HALO // 2 :]
            return summed * pltpu.reciprocal(1.0 + jnp.exp(-summed), approx=True)

        def field(p):
            pieces = [
                part[rows + top : rows + top + size, left : left + rows].astype(jnp.float32)
                for q, _, size, top, left in scalar_units(heads, rows, full)
                if q == p
            ]
            return jnp.concatenate(pieces, axis=0).astype(jnp.bfloat16)

        cumul = contract(ones, field(0), ((1,), (1,)))
        steps = contract(eye, field(1), ((1,), (1,)))
        middles = [
            cumul[b * BLOCK + BLOCK // 2 - 1 : b * BLOCK + BLOCK // 2] for b in range(blocks)
        ]
        middle = jnp.concatenate([jnp.broadcast_to(m, (BLOCK, heads)) for m in middles], axis=0)
        inward = jnp.concatenate(as_parts(steps * jnp.exp(middle - cumul), 2), axis=1)
        outward = jnp.concatenate(
            as_parts(
                jnp.concatenate(
                    [jnp.exp(cumul - middle)]
                    + [jnp.broadcast_to(jnp.exp(m), (16, heads)) for m in middles],
                    axis=0,
                ),
                2,
            ),
            axis=1,
        )
        outward_out[source] = outward
        scales[...] = contract(
            jnp.concatenate([inward, outward[:rows]], axis=0), expand, ((1,), (0,))
        )
        b_part, c_part = (
            jnp.concatenate(
                [activated(r, lane) for r in range(0, rows, STRIP)], axis=0
            ).astype(jnp.bfloat16)
            for lane in (width, width + STATE)
        )
        c_out[source] = c_part
        scores = contract(c_part, b_part, ((1,), (1,)))
        scores = jnp.where(lower, scores, 0.0).astype(jnp.bfloat16)
        for lane in range(0, width, LANES):
            at = slice(lane, lane + LANES)
            for r in range(0, rows, STRIP):
                x_conv = activated(r, lane)
                x_ref[r : r + STRIP, at] = x_conv
                scaled_ref[r : r + STRIP, at] = (x_conv * scales[r : r + STRIP, at]).astype(
                    jnp.bfloat16
                )
        for b in range(blocks):
            at = slice(b * BLOCK, (b + 1) * BLOCK)
            added = contract(b_part[at], scaled_ref[at], ((0,), (0,)))
            state[source, b * STATE : (b + 1) * STATE] = added.astype(jnp.bfloat16)
        intra = contract(scores, scaled_ref[...], ((1,), (0,)))
        pre[source] = (intra * scales[rows:] + skip_ref[...] * x_ref[...]).astype(jnp.bfloat16)


def carry_kernel(width, heads, whole_group, *refs):
    pre, state, c_part, outward, gain_ref = refs[:5]
    outs, (carry, scales, expand) = refs[5:-3], refs[-3:]
    rows = pre.shape[1]
    blocks = rows // BLOCK
    step = pl.program_id(0)

    @pl.when(step == 0)
    def _():
        carry[...] = jnp.zeros_like(carry)
        expand[...] = spread(heads)

    for half in range(PAIR):
        source = step * PAIR + half
        scales[half] = contract(outward[source], expand[...], ((1,), (0,)))
    held = []
    for half in range(PAIR):
        source = step * PAIR + half
        for b in range(blocks):
            middle_row = rows + 16 * b
            last_row = (b + 1) * BLOCK - 1
            now = carry[...] * scales[half, middle_row : middle_row + 1]
            held.append(now.astype(jnp.bfloat16))
            added = state[source, b * STATE : (b + 1) * STATE].astype(jnp.float32)
            carry[...] = (now + added) * scales[half, last_row : last_row + 1]
    for half in range(PAIR):
        source = step * PAIR + half
        for b in range(blocks):
            at = slice(b * BLOCK, (b + 1) * BLOCK)
            to = slice(half * rows + b * BLOCK, half * rows + (b + 1) * BLOCK)
            inter = contract(c_part[source, at], held[half * blocks + b], ((1,), (0,)))
            total = pre[source, at].astype(jnp.float32) + inter * scales[half, at]
            power = total[:, :LANES] * total[:, :LANES]
            for lane in range(LANES, width, LANES):
                power = power + total[:, lane : lane + LANES] * total[:, lane : lane + LANES]
            if whole_group:
                summed = jnp.sum(power, axis=1, keepdims=True)
                norm = lax.rsqrt(summed * (1.0 / GROUP_WIDTH) + EPS)
                outs[0][to] = (total * norm * gain_ref[...]).astype(jnp.bfloat16)
            else:
                outs[0][to] = total
                outs[1][to] = power


def per_device(inputs, key_query, conv_inputs, conv_kq, step_size, decay_log, skip_gain, norm_gain):
    peers = lax.axis_size("ctx")
    me = lax.axis_index("ctx")
    rows = inputs.shape[0]
    width = HEADS * HEAD_DIM // peers
    heads = HEADS // peers
    span = GROUP_WIDTH // width
    whole_group = span == 1
    blocks = rows // BLOCK
    full = width + 2 * STATE
    scalar_rows = scalar_units(heads, rows, full)[-1][3] + SUBLANES
    scale_rows = rows + 16 * blocks
    cycle = jnp.arange(peers, dtype=jnp.int32)
    owners = lax.rem(me + cycle, peers)
    sources = lax.rem(me + peers - cycle, peers)

    smem = pl.BlockSpec(memory_space=pltpu.SMEM)
    hbm = pl.BlockSpec(memory_space=pltpu.HBM)
    vmem = pl.BlockSpec(memory_space=pltpu.VMEM)
    params = pltpu.CompilerParams(vmem_limit_bytes=VMEM_LIMIT)

    def columns(a, first, size):
        return lax.dynamic_slice_in_dim(a, first, size, axis=1)

    def pack(codes):
        shape = jax.ShapeDtypeStruct((rows + scalar_rows, full), jnp.bfloat16)
        return pl.pallas_call(
            functools.partial(pack_kernel, peers, span, width, heads, codes),
            in_specs=[smem] + [hbm] * 4,
            out_specs=[vmem] * len(codes),
            out_shape=[shape] * len(codes),
            scratch_shapes=[
                pltpu.VMEM((FIELDS, rows, HEADS), jnp.float32),
                pltpu.VMEM((FIELDS, peers, heads, rows), jnp.float32),
                pltpu.VMEM(key_query.shape, jnp.bfloat16),
                pltpu.SemaphoreType.DMA((2, max(3, len(codes)))),
            ],
            compiler_params=pltpu.CompilerParams(vmem_limit_bytes=PACK_VMEM),
            cost_estimate=pl.CostEstimate(
                flops=0, bytes_accessed=4 * len(codes) * rows * full, transcendentals=0
            ),
            name="pack",
        )(owners, inputs, key_query, decay_log, step_size)

    codes = [code for code in ORDER if code < peers]
    codes += [code for code in range(1, peers) if code not in codes]
    parts = dict(zip(codes[:WINDOW], pack(codes[:WINDOW])))
    parts.update(zip(codes[WINDOW:] + [0], pack(codes[WINDOW:] + [0])))
    for i, code in enumerate(codes):
        pairs = [(j, (j + code) % peers) for j in range(peers)]
        message = parts[code]
        if i >= WINDOW:
            message, _ = lax.optimization_barrier((message, parts[codes[i - WINDOW]]))
        parts[code] = lax.ppermute(message, "ctx", pairs)

    group = me // span
    taps = jnp.concatenate(
        [
            columns(conv_inputs, me * width, width),
            columns(conv_kq, group * STATE, STATE),
            columns(conv_kq, (GROUPS + group) * STATE, STATE),
        ],
        axis=1,
    )
    skip = jnp.repeat(lax.dynamic_slice_in_dim(skip_gain, me * heads, heads), HEAD_DIM)[None]
    gain = columns(norm_gain[None], me * width, width)

    shapes = [
        (rows, width),
        (blocks * STATE, width),
        (rows, STATE),
        (scale_rows, 2 * heads),
    ]
    arrived = {0}
    pending = list(range(peers))
    stores = []
    for code in codes:
        arrived.add(code)
        ready = [k for k in pending if {k, (k + 1) % peers} <= arrived]
        pending = [k for k in pending if k not in ready]
        if not ready:
            continue
        count = len(ready)
        operands = []
        for k in ready:
            operands += [parts[k], parts[(k + 1) % peers]]
        stores = pl.pallas_call(
            functools.partial(local_kernel, width, heads, count, bool(stores)),
            in_specs=[smem] + [vmem] * (2 * count + 2 + len(stores)),
            out_specs=[vmem] * 4,
            out_shape=[jax.ShapeDtypeStruct((peers,) + shape, jnp.bfloat16) for shape in shapes],
            input_output_aliases={3 + 2 * count + i: i for i in range(len(stores))},
            scratch_shapes=[
                pltpu.VMEM((rows + HALO, full), jnp.bfloat16),
                pltpu.VMEM((rows, width), jnp.float32),
                pltpu.VMEM((rows, width), jnp.bfloat16),
                pltpu.VMEM((2 * rows, width), jnp.float32),
            ],
            compiler_params=params,
            cost_estimate=pl.CostEstimate(
                flops=2 * rows * count * width * 450,
                bytes_accessed=count * rows * width * 10,
                transcendentals=count * rows * full,
            ),
            name="local",
        )(jnp.stack([sources[k] for k in ready]), *operands, taps, skip, *stores)

    out = [((rows, width), jnp.bfloat16 if whole_group else jnp.float32)]
    if not whole_group:
        out.append(((rows, LANES), jnp.float32))
    results = pl.pallas_call(
        functools.partial(carry_kernel, width, heads, whole_group),
        grid=(peers // PAIR,),
        in_specs=[vmem] * 5,
        out_specs=[pl.BlockSpec((PAIR * shape[0], shape[1]), lambda i: (i, 0)) for shape, _ in out],
        out_shape=[
            jax.ShapeDtypeStruct((peers * shape[0], shape[1]), dtype) for shape, dtype in out
        ],
        scratch_shapes=[
            pltpu.VMEM((STATE, width), jnp.float32),
            pltpu.VMEM((PAIR, scale_rows, width), jnp.float32),
            pltpu.VMEM((2 * heads, width), jnp.bfloat16),
        ],
        compiler_params=params,
        cost_estimate=pl.CostEstimate(
            flops=2 * peers * rows * width * 150,
            bytes_accessed=peers * rows * width * 8,
            transcendentals=peers * rows,
        ),
        name="carry",
    )(*stores, gain)
    if whole_group:
        return results[0]
    total, power = results
    sharers = [list(range(i, i + span)) for i in range(0, peers, span)]
    summed = jnp.sum(power, axis=1, keepdims=True)
    summed = lax.psum(summed, "ctx", axis_index_groups=sharers)
    return (total * lax.rsqrt(summed * (1.0 / GROUP_WIDTH) + EPS) * gain).astype(jnp.bfloat16)


def solution(mesh):
    in_specs = (
        P(("dp", "ctx"), None),
        P(("dp", "ctx"), None),
        P(),
        P(),
        P(("dp", "ctx"), None),
        P(("dp", "ctx"), None),
        P(),
        P(),
    )
    out_specs = P("dp", "ctx")
    return jax.shard_map(
        per_device, mesh=mesh, in_specs=in_specs, out_specs=out_specs, check_vma=False
    )
```

profile of v0, /device:TPU:17, one launch (start us, length us, event | category | flops | bytes accessed | tf_op | source)
XLA Modules:
  0.0 139.2 jit_solution(10908503058530078212)
XLA Ops:
  0.0 0.0 copy-start
  0.0 0.5 compare_select_fusion.refs_0_
  0.6 0.0 copy-start.2
  0.6 4.0 %pack.3 = (bf16[264,1280]{1,0:T(8,128)(2,1)}, bf16[264,1280]{1,0:T(8,128)(2,1)}, bf16[264,1280]{1,0:T(8,128)(2,1)}) custom-call(s32[8]{0:T(128)} %compare_select_fusion.refs_0_, bf16[256,8192]{1,0:T(8,128)(2,1)} %refs_1_.3, bf16[256,2048]{1,0:T(8,128)(2,1)} %refs_2_.3, f32[256,128]{1,0:T(8,128)} %refs_3_.3, f32[256,128]{1,0:T(8,128)} %refs_4_.3), custom_call_target="tpu_custom_call" | custom-call | bytes 3932160 | tf_op jit(solution)/shard_map/pack/pallas_call | solution.py:257
  4.6 0.1 collective-permute-start.2
  4.7 2.2 %collective-permute-start.5 = (bf16[264,1280]{1,0:T(8,128)(2,1)}, bf16[264,1280]{1,0:T(8,128)(2,1)S(1)}, u32[]{:S(2)}, u32[]{:S(2)}) collective-permute-start(bf16[264,1280]{1,0:T(8,128)(2,1)} %get-tuple-element.49), channel_id=1, source_target_pairs={{0,1},{1,2},{2,3},{3,4},{4,5},{5,6},{6,7},{7,0},{8,9},{9,10},{10,1... | collective-permute-start | bytes 2027528 | tf_op jit(solution)/shard_map/ppermute | solution.py:284
  6.8 0.0 collective-permute-start
  6.9 4.6 %pack.2 = (bf16[264,1280]{1,0:T(8,128)(2,1)}, bf16[264,1280]{1,0:T(8,128)(2,1)}, bf16[264,1280]{1,0:T(8,128)(2,1)}, bf16[264,1280]{1,0:T(8,128)(2,1)}, bf16[264,1280]{1,0:T(8,128)(2,1)}) custom-call(s32[8]{0:T(128)} %compare_select_fusion.refs_0_, bf16[256,8192]{1,0:T(8,128)(2,1)} %refs_1_.3, bf16[256,2048]{1,0:T(8,128)(2,1)} %refs_2_.3, ...), custom_call_target="tpu_custom_call" | custom-call | bytes 6553600 | tf_op jit(solution)/shard_map/pack/pallas_call | solution.py:257
  11.5 29.4 %collective-permute-done.2.refs_2_.refs_1_ = bf16[264,1280]{1,0:T(8,128)(2,1)S(1)} collective-permute-done((bf16[264,1280]{1,0:T(8,128)(2,1)}, bf16[264,1280]{1,0:T(8,128)(2,1)S(1)}, u32[]{:S(2)}, u32[]{:S(2)}) %collective-permute-start.2) | collective-permute-done | bytes 675872 | tf_op jit(solution)/shard_map/ppermute | solution.py:284
  40.9 4.1 %collective-permute-start.3 = (bf16[264,1280]{1,0:T(8,128)(2,1)}, bf16[264,1280]{1,0:T(8,128)(2,1)S(1)}, u32[]{:S(2)}, u32[]{:S(2)}) collective-permute-start(bf16[264,1280]{1,0:T(8,128)(2,1)} %get-tuple-element.47), channel_id=1, source_target_pairs={{0,3},{1,4},{2,5},{3,6},{4,7},{5,0},{6,1},{7,2},{8,11},{9,12},{10,... | collective-permute-start | bytes 2027528 | tf_op jit(solution)/shard_map/ppermute | solution.py:284
  45.0 0.0 copy-done
  45.0 0.0 collective-permute-done.5.refs_2_.refs_1_
  45.0 0.9 collective-permute-start.6
  45.9 0.0 collective-permute-done.refs_1_.refs_4_
  45.9 21.3 %collective-permute-start.1 = (bf16[264,1280]{1,0:T(8,128)(2,1)}, bf16[264,1280]{1,0:T(8,128)(2,1)S(1)}, u32[]{:S(2)}, u32[]{:S(2)}) collective-permute-start(bf16[264,1280]{1,0:T(8,128)(2,1)} %get-tuple-element.43), channel_id=1, source_target_pairs={{0,5},{1,6},{2,7},{3,0},{4,1},{5,2},{6,3},{7,4},{8,13},{9,14},{10,... | collective-permute-start | bytes 2027528 | tf_op jit(solution)/shard_map/ppermute | solution.py:284
  67.2 0.7 fusion.2
  67.8 0.0 copy-done.2
  67.8 0.1 dynamic_slice.18
  67.9 0.1 broadcast_in_dim.4
  68.0 0.1 broadcast_in_dim_reshape.3.refs_4_.refs_6_
  68.1 0.7 dynamic-slice.3
  68.8 21.4 %collective-permute-done.3.refs_1_.refs_4_ = bf16[264,1280]{1,0:T(8,128)(2,1)S(1)} collective-permute-done((bf16[264,1280]{1,0:T(8,128)(2,1)}, bf16[264,1280]{1,0:T(8,128)(2,1)S(1)}, u32[]{:S(2)}, u32[]{:S(2)}) %collective-permute-start.3) | collective-permute-done | bytes 675872 | tf_op jit(solution)/shard_map/ppermute | solution.py:284
  90.1 9.8 %collective-permute-start.4 = (bf16[264,1280]{1,0:T(8,128)(2,1)}, bf16[264,1280]{1,0:T(8,128)(2,1)S(1)}, u32[]{:S(2)}, u32[]{:S(2)}) collective-permute-start(bf16[264,1280]{1,0:T(8,128)(2,1)} %get-tuple-element.48), channel_id=1, source_target_pairs={{0,6},{1,7},{2,0},{3,1},{4,2},{5,3},{6,4},{7,5},{8,14},{9,15},{10,... | collective-permute-start | bytes 2027528 | tf_op jit(solution)/shard_map/ppermute | solution.py:284
  99.9 0.7 constant_dynamic-slice_fusion.1
  100.6 0.1 fusion.3
  100.7 0.0 copy-start.1
  100.7 1.1 copy-done.1
  101.8 2.3 %local.6 = (bf16[8,256,1024]{2,1,0:T(8,128)(2,1)S(1)}, bf16[8,256,1024]{2,1,0:T(8,128)(2,1)S(1)}, bf16[8,256,128]{2,1,0:T(8,128)(2,1)S(1)}, bf16[8,288,32]{2,1,0:T(8,128)(2,1)S(1)}) custom-call(s32[1]{0:T(128)} %get-tuple-element.79.refs_0_, bf16[264,1280]{1,0:T(8,128)(2,1)S(1)} %copy-done.1, bf16[264,1280]{1,0:T(8,128)(2,1)S(1)} %collective-permute-done.5.refs_2_.refs_1_, ...), custom_call_target="tpu_custom_call" | custom-call | flops 235929600 | bytes 2621440 | tf_op jit(solution)/shard_map/local/pallas_call | solution.py:317
  104.1 2.3 %local.7 = (bf16[8,256,1024]{2,1,0:T(8,128)(2,1)S(1)}, bf16[8,256,1024]{2,1,0:T(8,128)(2,1)S(1)}, bf16[8,256,128]{2,1,0:T(8,128)(2,1)S(1)}, bf16[8,288,32]{2,1,0:T(8,128)(2,1)S(1)}) custom-call(s32[1]{0:T(128)} %get-tuple-element.80.refs_0_, ...), custom_call_target="tpu_custom_call", output_to_operand_aliasing={{0}: (5, {}), {1}: (6, {}), {2}: (7, {}), {3}: (8, {})} | custom-call | flops 235929600 | bytes 2621440 | tf_op jit(solution)/shard_map/local/pallas_call | solution.py:317
  106.3 2.3 %local.8 = (bf16[8,256,1024]{2,1,0:T(8,128)(2,1)S(1)}, bf16[8,256,1024]{2,1,0:T(8,128)(2,1)S(1)}, bf16[8,256,128]{2,1,0:T(8,128)(2,1)S(1)}, bf16[8,288,32]{2,1,0:T(8,128)(2,1)S(1)}) custom-call(s32[1]{0:T(128)} %get-tuple-element.81.refs_0_, ...), custom_call_target="tpu_custom_call", output_to_operand_aliasing={{0}: (5, {}), {1}: (6, {}), {2}: (7, {}), {3}: (8, {})} | custom-call | flops 235929600 | bytes 2621440 | tf_op jit(solution)/shard_map/local/pallas_call | solution.py:317
  108.7 13.4 %collective-permute-done.6.refs_2_.refs_3_ = bf16[264,1280]{1,0:T(8,128)(2,1)} collective-permute-done((bf16[264,1280]{1,0:T(8,128)(2,1)}, bf16[264,1280]{1,0:T(8,128)(2,1)}, u32[]{:S(2)}, u32[]{:S(2)}) %collective-permute-start.6) | collective-permute-done | bytes 675872 | tf_op jit(solution)/shard_map/ppermute | solution.py:284
  122.1 4.6 %local.9 = (bf16[8,256,1024]{2,1,0:T(8,128)(2,1)S(1)}, bf16[8,256,1024]{2,1,0:T(8,128)(2,1)S(1)}, bf16[8,256,128]{2,1,0:T(8,128)(2,1)S(1)}, bf16[8,288,32]{2,1,0:T(8,128)(2,1)S(1)}) custom-call(s32[2]{0:T(128)S(1)} %get-tuple-element.83.refs_0_, ...), custom_call_target="tpu_custom_call", output_to_operand_aliasing={{0}: (7, {}), {1}: (8, {}), {2}: (9, {}), {3}: (10, {})} | custom-call | flops 471859200 | bytes 5242880 | tf_op jit(solution)/shard_map/local/pallas_call | solution.py:317
  126.7 0.0 collective-permute-done.1.refs_2_.refs_1_
  126.7 2.2 %local.10 = (bf16[8,256,1024]{2,1,0:T(8,128)(2,1)S(1)}, bf16[8,256,1024]{2,1,0:T(8,128)(2,1)S(1)}, bf16[8,256,128]{2,1,0:T(8,128)(2,1)S(1)}, bf16[8,288,32]{2,1,0:T(8,128)(2,1)S(1)}) custom-call(s32[1]{0:T(128)} %get-tuple-element.82.refs_0_, ...), custom_call_target="tpu_custom_call", output_to_operand_aliasing={{0}: (5, {}), {1}: (6, {}), {2}: (7, {}), {3}: (8, {})} | custom-call | flops 235929600 | bytes 2621440 | tf_op jit(solution)/shard_map/local/pallas_call | solution.py:317
  128.9 0.0 collective-permute-done.4.refs_2_.refs_3_
  128.9 3.8 %local.11 = (bf16[8,256,1024]{2,1,0:T(8,128)(2,1)S(1)}, bf16[8,256,1024]{2,1,0:T(8,128)(2,1)S(1)}, bf16[8,256,128]{2,1,0:T(8,128)(2,1)S(1)}, bf16[8,288,32]{2,1,0:T(8,128)(2,1)S(1)}) custom-call(s32[2]{0:T(128)S(1)} %get-tuple-element.84.refs_0_, ...), custom_call_target="tpu_custom_call", output_to_operand_aliasing={{0}: (7, {}), {1}: (8, {}), {2}: (9, {}), {3}: (10, {})} | custom-call | flops 471859200 | bytes 5242880 | tf_op jit(solution)/shard_map/local/pallas_call | solution.py:317
  132.7 6.5 %carry.1 = bf16[2048,1024]{1,0:T(8,128)(2,1)} custom-call(bf16[8,256,1024]{2,1,0:T(8,128)(2,1)S(1)} %get-tuple-element.73.refs_0_, bf16[8,256,1024]{2,1,0:T(8,128)(2,1)S(1)} %get-tuple-element.74.refs_1_, bf16[8,256,128]{2,1,0:T(8,128)(2,1)S(1)} %get-tuple-element.75.refs_2_, bf16[8,288,32]{2,1,0:T(8,128)(2,1)S(1)} %get-tuple-element.76.refs_3_, ...), custom_call_target="tpu_custom_call" | custom-call | flops 629145600 | bytes 16777216 | tf_op jit(solution)/shard_map/carry/pallas_call | solution.py:341
  (3 shorter events, 0.0 us)
Async XLA Ops:
  0.0 45.0 %copy-start = (f32[4,8192]{1,0:T(4,128)S(1)}, f32[4,8192]{1,0:T(4,128)}, u32[]{:S(2)}) copy-start(f32[4,8192]{1,0:T(4,128)} %param.10) | copy-start | bytes 393220
  0.6 67.3 %copy-start.2 = (f32[128]{0:T(128)S(1)}, f32[128]{0:T(128)}, u32[]{:S(2)}) copy-start(f32[128]{0:T(128)} %param.14) | copy-start | bytes 1540
  4.6 36.3 %collective-permute-start.2 = (bf16[264,1280]{1,0:T(8,128)(2,1)}, bf16[264,1280]{1,0:T(8,128)(2,1)S(1)}, u32[]{:S(2)}, u32[]{:S(2)}) collective-permute-start(bf16[264,1280]{1,0:T(8,128)(2,1)} %get-tuple-element.46), channel_id=1, source_target_pairs={{0,4},{1,5},{2,6},{3,7},{4,0},{5,1},{6,2},{7,3},{8,12},{9,13},{10,... | collective-permute-start | bytes 2027528 | tf_op jit(solution)/shard_map/ppermute | solution.py:284
  4.7 40.3 %collective-permute-start.5 = (bf16[264,1280]{1,0:T(8,128)(2,1)}, bf16[264,1280]{1,0:T(8,128)(2,1)S(1)}, u32[]{:S(2)}, u32[]{:S(2)}) collective-permute-start(bf16[264,1280]{1,0:T(8,128)(2,1)} %get-tuple-element.49), channel_id=1, source_target_pairs={{0,1},{1,2},{2,3},{3,4},{4,5},{5,6},{6,7},{7,0},{8,9},{9,10},{10,1... | collective-permute-start | bytes 2027528 | tf_op jit(solution)/shard_map/ppermute | solution.py:284
  6.8 39.0 %collective-permute-start = (bf16[264,1280]{1,0:T(8,128)(2,1)}, bf16[264,1280]{1,0:T(8,128)(2,1)S(1)}, u32[]{:S(2)}, u32[]{:S(2)}) collective-permute-start(bf16[264,1280]{1,0:T(8,128)(2,1)} %get-tuple-element.42), channel_id=1, source_target_pairs={{0,7},{1,0},{2,1},{3,2},{4,3},{5,4},{6,5},{7,6},{8,15},{9,8},{10,9... | collective-permute-start | bytes 2027528 | tf_op jit(solution)/shard_map/ppermute | solution.py:284
  40.9 49.3 %collective-permute-start.3 = (bf16[264,1280]{1,0:T(8,128)(2,1)}, bf16[264,1280]{1,0:T(8,128)(2,1)S(1)}, u32[]{:S(2)}, u32[]{:S(2)}) collective-permute-start(bf16[264,1280]{1,0:T(8,128)(2,1)} %get-tuple-element.47), channel_id=1, source_target_pairs={{0,3},{1,4},{2,5},{3,6},{4,7},{5,0},{6,1},{7,2},{8,11},{9,12},{10,... | collective-permute-start | bytes 2027528 | tf_op jit(solution)/shard_map/ppermute | solution.py:284
  45.0 77.1 %collective-permute-start.6 = (bf16[264,1280]{1,0:T(8,128)(2,1)}, bf16[264,1280]{1,0:T(8,128)(2,1)}, u32[]{:S(2)}, u32[]{:S(2)}) collective-permute-start(bf16[264,1280]{1,0:T(8,128)(2,1)} %get-tuple-element.51), channel_id=1, source_target_pairs={{0,2},{1,3},{2,4},{3,5},{4,6},{5,7},{6,0},{7,1},{8,10},{9,11},{10,... | collective-permute-start | bytes 2027528 | tf_op jit(solution)/shard_map/ppermute | solution.py:284
  45.9 80.8 %collective-permute-start.1 = (bf16[264,1280]{1,0:T(8,128)(2,1)}, bf16[264,1280]{1,0:T(8,128)(2,1)S(1)}, u32[]{:S(2)}, u32[]{:S(2)}) collective-permute-start(bf16[264,1280]{1,0:T(8,128)(2,1)} %get-tuple-element.43), channel_id=1, source_target_pairs={{0,5},{1,6},{2,7},{3,0},{4,1},{5,2},{6,3},{7,4},{8,13},{9,14},{10,... | collective-permute-start | bytes 2027528 | tf_op jit(solution)/shard_map/ppermute | solution.py:284
  90.1 38.8 %collective-permute-start.4 = (bf16[264,1280]{1,0:T(8,128)(2,1)}, bf16[264,1280]{1,0:T(8,128)(2,1)S(1)}, u32[]{:S(2)}, u32[]{:S(2)}) collective-permute-start(bf16[264,1280]{1,0:T(8,128)(2,1)} %get-tuple-element.48), channel_id=1, source_target_pairs={{0,6},{1,7},{2,0},{3,1},{4,2},{5,3},{6,4},{7,5},{8,14},{9,15},{10,... | collective-permute-start | bytes 2027528 | tf_op jit(solution)/shard_map/ppermute | solution.py:284
  100.7 1.1 copy-start.1
where the time goes:
time: 140 us; the launch traced here: 139 us
  waiting for transfers between devices  64.2 us (46%)
  starting transfers between devices  38.3 us (27%)
  Pallas kernels  32.7 us (23%)
  local copies, waits for them, and re-layouts  3.47 us (2%)
    ppermute x7, waiting for transfers between devices, per_device(): parts[code] = lax.ppermute(message, 'ctx', pairs)  64.2 us
    ppermute x7, starting transfers between devices, per_device(): parts[code] = lax.ppermute(message, 'ctx', pairs)  38.3 us
    pallas_call x6, Pallas kernels, per_device(): pl.pallas_call(functools.partial(local_kernel, width, heads, count, bool(...  17.5 us
    pallas_call x2, Pallas kernels, pack(): pl.pallas_call(functools.partial(pack_kernel, peers, span, width, heads,...  8.65 us
    pallas_call x1, Pallas kernels, per_device(): pl.pallas_call(functools.partial(carry_kernel, width, heads, whole_group)...  6.5 us
  transfers between devices with their start and end apart: 7, of which 3 were waited for; matrix products, arithmetic and copies ran while one was open for 2% of the time, Pallas kernels for 13%

commit v1 on v0

--- a/solution.py
+++ b/solution.py
@@ -21,8 +21,8 @@
 FIELDS = 2
 STRIP = 64
 PAIR = 2
-WINDOW = 3
-ORDER = (4, 1, 7, 3, 2, 5, 6)
+WINDOW = 5
+ORDER = (4, 1, 3, 7, 5, 2, 6)
 PACK_VMEM = 58 * 1024 * 1024
 VMEM_LIMIT = 28 * 1024 * 1024
 
@@ -100,9 +100,9 @@
     source_ref = refs[0]
     parts = refs[1 : 1 + 2 * count]
     taps_ref, skip_ref = refs[1 + 2 * count : 3 + 2 * count]
-    refs = refs[3 + 2 * count + (4 if chained else 0) :]
-    pre, state, c_out, outward_out = refs[:4]
-    wide, x_ref, scaled_ref, scales = refs[4:]
+    refs = refs[3 + 2 * count + (5 if chained else 0) :]
+    pre, state, c_out, fade_out, edge_out = refs[:5]
+    wide, x_ref, scaled_ref, scales = refs[5:]
     rows = x_ref.shape[0]
     blocks = rows // BLOCK
     full = width + 2 * STATE
@@ -155,10 +155,16 @@
             ),
             axis=1,
         )
-        outward_out[source] = outward
         scales[...] = contract(
-            jnp.concatenate([inward, outward[:rows]], axis=0), expand, ((1,), (0,))
-        )
+            jnp.concatenate([inward, outward], axis=0), expand, ((1,), (0,))
+        )
+        edges = []
+        for b in range(blocks):
+            last_row = rows + (b + 1) * BLOCK - 1
+            middle_row = 2 * rows + 16 * b
+            edges += [scales[middle_row : middle_row + 1], scales[last_row : last_row + 1]]
+        edge_out[source, 0 : 2 * blocks] = jnp.concatenate(edges, axis=0)
+        fade_out[source] = scales[rows : 2 * rows].astype(jnp.bfloat16)
         b_part, c_part = (
             jnp.concatenate(
                 [activated(r, lane) for r in range(0, rows, STRIP)], axis=0
@@ -181,12 +187,12 @@
             added = contract(b_part[at], scaled_ref[at], ((0,), (0,)))
             state[source, b * STATE : (b + 1) * STATE] = added.astype(jnp.bfloat16)
         intra = contract(scores, scaled_ref[...], ((1,), (0,)))
-        pre[source] = (intra * scales[rows:] + skip_ref[...] * x_ref[...]).astype(jnp.bfloat16)
-
-
-def carry_kernel(width, heads, whole_group, *refs):
-    pre, state, c_part, outward, gain_ref = refs[:5]
-    outs, (carry, scales, expand) = refs[5:-3], refs[-3:]
+        pre[source] = (intra * scales[rows : 2 * rows] + skip_ref[...] * x_ref[...]).astype(jnp.bfloat16)
+
+
+def carry_kernel(width, whole_group, *refs):
+    pre, state, c_part, fade, edge, gain_ref = refs[:6]
+    outs, carry = refs[6:-1], refs[-1]
     rows = pre.shape[1]
     blocks = rows // BLOCK
     step = pl.program_id(0)
@@ -194,28 +200,24 @@
     @pl.when(step == 0)
     def _():
         carry[...] = jnp.zeros_like(carry)
-        expand[...] = spread(heads)
-
-    for half in range(PAIR):
-        source = step * PAIR + half
-        scales[half] = contract(outward[source], expand[...], ((1,), (0,)))
+
     held = []
     for half in range(PAIR):
         source = step * PAIR + half
         for b in range(blocks):
-            middle_row = rows + 16 * b
-            last_row = (b + 1) * BLOCK - 1
-            now = carry[...] * scales[half, middle_row : middle_row + 1]
+            now = carry[...] * edge[source, 2 * b : 2 * b + 1]
             held.append(now.astype(jnp.bfloat16))
             added = state[source, b * STATE : (b + 1) * STATE].astype(jnp.float32)
-            carry[...] = (now + added) * scales[half, last_row : last_row + 1]
+            carry[...] = (now + added) * edge[source, 2 * b + 1 : 2 * b + 2]
     for half in range(PAIR):
         source = step * PAIR + half
         for b in range(blocks):
             at = slice(b * BLOCK, (b + 1) * BLOCK)
             to = slice(half * rows + b * BLOCK, half * rows + (b + 1) * BLOCK)
             inter = contract(c_part[source, at], held[half * blocks + b], ((1,), (0,)))
-            total = pre[source, at].astype(jnp.float32) + inter * scales[half, at]
+            total = pre[source, at].astype(jnp.float32) + inter * fade[source, at].astype(
+                jnp.float32
+            )
             power = total[:, :LANES] * total[:, :LANES]
             for lane in range(LANES, width, LANES):
                 power = power + total[:, lane : lane + LANES] * total[:, lane : lane + LANES]
@@ -296,10 +298,11 @@
     gain = columns(norm_gain[None], me * width, width)
 
     shapes = [
-        (rows, width),
-        (blocks * STATE, width),
-        (rows, STATE),
-        (scale_rows, 2 * heads),
+        ((rows, width), jnp.bfloat16),
+        ((blocks * STATE, width), jnp.bfloat16),
+        ((rows, STATE), jnp.bfloat16),
+        ((rows, width), jnp.bfloat16),
+        ((2 * blocks, width), jnp.float32),
     ]
     arrived = {0}
     pending = list(range(peers))
@@ -317,14 +320,14 @@
         stores = pl.pallas_call(
             functools.partial(local_kernel, width, heads, count, bool(stores)),
             in_specs=[smem] + [vmem] * (2 * count + 2 + len(stores)),
-            out_specs=[vmem] * 4,
-            out_shape=[jax.ShapeDtypeStruct((peers,) + shape, jnp.bfloat16) for shape in shapes],
+            out_specs=[vmem] * len(shapes),
+            out_shape=[jax.ShapeDtypeStruct((peers,) + shape, dtype) for shape, dtype in shapes],
             input_output_aliases={3 + 2 * count + i: i for i in range(len(stores))},
             scratch_shapes=[
                 pltpu.VMEM((rows + HALO, full), jnp.bfloat16),
                 pltpu.VMEM((rows, width), jnp.float32),
                 pltpu.VMEM((rows, width), jnp.bfloat16),
-                pltpu.VMEM((2 * rows, width), jnp.float32),
+                pltpu.VMEM((rows + scale_rows, width), jnp.float32),
             ],
             compiler_params=params,
             cost_estimate=pl.CostEstimate(
@@ -339,17 +342,15 @@
     if not whole_group:
         out.append(((rows, LANES), jnp.float32))
     results = pl.pallas_call(
-        functools.partial(carry_kernel, width, heads, whole_group),
+        functools.partial(carry_kernel, width, whole_group),
         grid=(peers // PAIR,),
-        in_specs=[vmem] * 5,
+        in_specs=[vmem] * (len(shapes) + 1),
         out_specs=[pl.BlockSpec((PAIR * shape[0], shape[1]), lambda i: (i, 0)) for shape, _ in out],
         out_shape=[
             jax.ShapeDtypeStruct((peers * shape[0], shape[1]), dtype) for shape, dtype in out
         ],
         scratch_shapes=[
             pltpu.VMEM((STATE, width), jnp.float32),
-            pltpu.VMEM((PAIR, scale_rows, width), jnp.float32),
-            pltpu.VMEM((2 * heads, width), jnp.bfloat16),
         ],
         compiler_params=params,
         cost_estimate=pl.CostEstimate(

time: 140 us -> 139 us (level)
  the two profiles are of different devices: /device:TPU:17 before, /device:TPU:12 now
where the time goes in v1:
time: 139 us; the launch traced here: 138 us
  waiting for transfers between devices  64.8 us (47%)
  starting transfers between devices  36.1 us (26%)
  Pallas kernels  32.8 us (24%)
  local copies, waits for them, and re-layouts  3.47 us (2%)
    ppermute x7, waiting for transfers between devices, per_device(): parts[code] = lax.ppermute(message, 'ctx', pairs)  64.8 us
    ppermute x7, starting transfers between devices, per_device(): parts[code] = lax.ppermute(message, 'ctx', pairs)  36.1 us
    pallas_call x6, Pallas kernels, per_device(): pl.pallas_call(functools.partial(local_kernel, width, heads, count, bool(...  18.8 us
    pallas_call x2, Pallas kernels, pack(): pl.pallas_call(functools.partial(pack_kernel, peers, span, width, heads,...  8.59 us
    pallas_call x1, Pallas kernels, per_device(): pl.pallas_call(functools.partial(carry_kernel, width, whole_group), grid=...  5.45 us
  transfers between devices with their start and end apart: 7, of which 4 were waited for; matrix products, arithmetic and copies ran while one was open for 2% of the time, Pallas kernels for 14%

profile of v1, /device:TPU:12, one launch (start us, length us, event | category | flops | bytes accessed | tf_op | source)
XLA Modules:
  0.0 137.9 jit_solution(3164396072804230732)
XLA Ops:
  0.0 0.0 copy-start
  0.0 0.6 compare_select_fusion.refs_0_
  0.6 0.0 copy-start.3
  0.6 4.8 %pack.2 = (bf16[264,1280]{1,0:T(8,128)(2,1)}, bf16[264,1280]{1,0:T(8,128)(2,1)}, bf16[264,1280]{1,0:T(8,128)(2,1)}, bf16[264,1280]{1,0:T(8,128)(2,1)}, bf16[264,1280]{1,0:T(8,128)(2,1)}) custom-call(s32[8]{0:T(128)} %compare_select_fusion.refs_0_, bf16[256,8192]{1,0:T(8,128)(2,1)} %refs_1_.3, bf16[256,2048]{1,0:T(8,128)(2,1)} %refs_2_.3, ...), custom_call_target="tpu_custom_call" | custom-call | bytes 6553600 | tf_op jit(solution)/shard_map/pack/pallas_call | solution.py:259
  5.4 2.7 %collective-permute-start.4 = (bf16[264,1280]{1,0:T(8,128)(2,1)}, bf16[264,1280]{1,0:T(8,128)(2,1)S(1)}, u32[]{:S(2)}, u32[]{:S(2)}) collective-permute-start(bf16[264,1280]{1,0:T(8,128)(2,1)} %get-tuple-element.51), channel_id=1, source_target_pairs={{0,4},{1,5},{2,6},{3,7},{4,0},{5,1},{6,2},{7,3},{8,12},{9,13},{10,... | collective-permute-start | bytes 2027528 | tf_op jit(solution)/shard_map/ppermute | solution.py:286
  8.0 0.0 collective-permute-start.1
  8.0 0.6 collective-permute-start.6
  8.6 1.1 collective-permute-start.3
  9.8 2.5 %collective-permute-start = (bf16[264,1280]{1,0:T(8,128)(2,1)}, bf16[264,1280]{1,0:T(8,128)(2,1)S(1)}, u32[]{:S(2)}, u32[]{:S(2)}) collective-permute-start(bf16[264,1280]{1,0:T(8,128)(2,1)} %get-tuple-element.45), channel_id=1, source_target_pairs={{0,5},{1,6},{2,7},{3,0},{4,1},{5,2},{6,3},{7,4},{8,13},{9,14},{10,... | collective-permute-start | bytes 2027528 | tf_op jit(solution)/shard_map/ppermute | solution.py:286
  12.2 3.8 %pack.3 = (bf16[264,1280]{1,0:T(8,128)(2,1)}, bf16[264,1280]{1,0:T(8,128)(2,1)}, bf16[264,1280]{1,0:T(8,128)(2,1)}) custom-call(s32[8]{0:T(128)} %compare_select_fusion.refs_0_, bf16[256,8192]{1,0:T(8,128)(2,1)} %refs_1_.3, bf16[256,2048]{1,0:T(8,128)(2,1)} %refs_2_.3, f32[256,128]{1,0:T(8,128)} %refs_3_.3, f32[256,128]{1,0:T(8,128)} %refs_4_.3), custom_call_target="tpu_custom_call" | custom-call | bytes 3932160 | tf_op jit(solution)/shard_map/pack/pallas_call | solution.py:259
  16.1 0.0 copy-done
  16.1 22.1 %collective-permute-done.4.refs_2_.refs_1_ = bf16[264,1280]{1,0:T(8,128)(2,1)S(1)} collective-permute-done((bf16[264,1280]{1,0:T(8,128)(2,1)}, bf16[264,1280]{1,0:T(8,128)(2,1)S(1)}, u32[]{:S(2)}, u32[]{:S(2)}) %collective-permute-start.4) | collective-permute-done | bytes 675872 | tf_op jit(solution)/shard_map/ppermute | solution.py:286
  38.2 27.0 %collective-permute-start.5 = (bf16[264,1280]{1,0:T(8,128)(2,1)}, bf16[264,1280]{1,0:T(8,128)(2,1)S(1)}, u32[]{:S(2)}, u32[]{:S(2)}) collective-permute-start(bf16[264,1280]{1,0:T(8,128)(2,1)} %get-tuple-element.52), channel_id=1, source_target_pairs={{0,2},{1,3},{2,4},{3,5},{4,6},{5,7},{6,0},{7,1},{8,10},{9,11},{10,... | collective-permute-start | bytes 2027528 | tf_op jit(solution)/shard_map/ppermute | solution.py:286
  65.2 0.7 fusion.2
  65.8 0.0 copy-done.3
  65.8 0.1 dynamic_slice.18
  65.9 0.1 broadcast_in_dim.4
  66.0 0.1 broadcast_in_dim_reshape.3.refs_4_.refs_6_
  66.1 0.7 dynamic-slice.3
  66.8 0.0 collective-permute-done.1.refs_2_.refs_1_
  66.8 2.3 %collective-permute-start.2 = (bf16[264,1280]{1,0:T(8,128)(2,1)}, bf16[264,1280]{1,0:T(8,128)(2,1)S(1)}, u32[]{:S(2)}, u32[]{:S(2)}) collective-permute-start(bf16[264,1280]{1,0:T(8,128)(2,1)} %get-tuple-element.48), channel_id=1, source_target_pairs={{0,6},{1,7},{2,0},{3,1},{4,2},{5,3},{6,4},{7,5},{8,14},{9,15},{10,... | collective-permute-start | bytes 2027528 | tf_op jit(solution)/shard_map/ppermute | solution.py:286
  69.0 0.7 constant_dynamic-slice_fusion.1
  69.7 0.1 fusion.3
  69.8 0.0 copy-start.1
  69.8 1.1 copy-done.1
  70.9 3.4 %local.6 = (bf16[8,256,1024]{2,1,0:T(8,128)(2,1)S(1)}, bf16[8,256,1024]{2,1,0:T(8,128)(2,1)S(1)}, bf16[8,256,128]{2,1,0:T(8,128)(2,1)S(1)}, bf16[8,256,1024]{2,1,0:T(8,128)(2,1)S(1)}, f32[8,4,1024]{2,1,0:T(4,128)S(1)}) custom-call(s32[1]{0:T(128)} %get-tuple-element.87.refs_0_, bf16[264,1280]{1,0:T(8,128)(2,1)S(1)} %copy-done.1, ...), custom_call_target="tpu_custom_call" | custom-call | flops 235929600 | bytes 2621440 | tf_op jit(solution)/shard_map/local/pallas_call | solution.py:320
  74.3 8.3 %collective-permute-done.6.refs_1_.refs_4_ = bf16[264,1280]{1,0:T(8,128)(2,1)S(1)} collective-permute-done((bf16[264,1280]{1,0:T(8,128)(2,1)}, bf16[264,1280]{1,0:T(8,128)(2,1)S(1)}, u32[]{:S(2)}, u32[]{:S(2)}) %collective-permute-start.6) | collective-permute-done | bytes 675872 | tf_op jit(solution)/shard_map/ppermute | solution.py:286
  82.6 0.0 copy-start.2
  82.6 2.4 %local.7 = (bf16[8,256,1024]{2,1,0:T(8,128)(2,1)S(1)}, bf16[8,256,1024]{2,1,0:T(8,128)(2,1)S(1)}, bf16[8,256,128]{2,1,0:T(8,128)(2,1)S(1)}, bf16[8,256,1024]{2,1,0:T(8,128)(2,1)S(1)}, f32[8,4,1024]{2,1,0:T(4,128)S(1)}) custom-call(s32[1]{0:T(128)} %get-tuple-element.88.refs_0_, ...), custom_call_target="tpu_custom_call", output_to_operand_aliasing={{0}: (5, {}), {1}: (6, {}), {2}: (7, {}), {3}: (8, {}), {4}... | custom-call | flops 235929600 | bytes 2621440 | tf_op jit(solution)/shard_map/local/pallas_call | solution.py:320
  85.0 0.0 collective-permute-done.3.refs_1_.refs_4_
  85.0 0.0 copy-done.2
  85.0 2.2 %local.8 = (bf16[8,256,1024]{2,1,0:T(8,128)(2,1)S(1)}, bf16[8,256,1024]{2,1,0:T(8,128)(2,1)S(1)}, bf16[8,256,128]{2,1,0:T(8,128)(2,1)S(1)}, bf16[8,256,1024]{2,1,0:T(8,128)(2,1)S(1)}, f32[8,4,1024]{2,1,0:T(4,128)S(1)}) custom-call(s32[1]{0:T(128)} %get-tuple-element.89.refs_0_, ...), custom_call_target="tpu_custom_call", output_to_operand_aliasing={{0}: (5, {}), {1}: (6, {}), {2}: (7, {}), {3}: (8, {}), {4}... | custom-call | flops 235929600 | bytes 2621440 | tf_op jit(solution)/shard_map/local/pallas_call | solution.py:320
  87.3 22.4 %collective-permute-done.refs_2_.refs_1_ = bf16[264,1280]{1,0:T(8,128)(2,1)S(1)} collective-permute-done((bf16[264,1280]{1,0:T(8,128)(2,1)}, bf16[264,1280]{1,0:T(8,128)(2,1)S(1)}, u32[]{:S(2)}, u32[]{:S(2)}) %collective-permute-start) | collective-permute-done | bytes 675872 | tf_op jit(solution)/shard_map/ppermute | solution.py:286
  109.7 2.4 %local.9 = (bf16[8,256,1024]{2,1,0:T(8,128)(2,1)S(1)}, bf16[8,256,1024]{2,1,0:T(8,128)(2,1)S(1)}, bf16[8,256,128]{2,1,0:T(8,128)(2,1)S(1)}, bf16[8,256,1024]{2,1,0:T(8,128)(2,1)S(1)}, f32[8,4,1024]{2,1,0:T(4,128)S(1)}) custom-call(s32[1]{0:T(128)} %get-tuple-element.90.refs_0_, ...), custom_call_target="tpu_custom_call", output_to_operand_aliasing={{0}: (5, {}), {1}: (6, {}), {2}: (7, {}), {3}: (8, {}), {4}... | custom-call | flops 235929600 | bytes 2621440 | tf_op jit(solution)/shard_map/local/pallas_call | solution.py:320
  112.1 12.0 %collective-permute-done.5.refs_2_.refs_3_ = bf16[264,1280]{1,0:T(8,128)(2,1)S(1)} collective-permute-done((bf16[264,1280]{1,0:T(8,128)(2,1)}, bf16[264,1280]{1,0:T(8,128)(2,1)S(1)}, u32[]{:S(2)}, u32[]{:S(2)}) %collective-permute-start.5) | collective-permute-done | bytes 675872 | tf_op jit(solution)/shard_map/ppermute | solution.py:286
  124.1 4.4 %local.10 = (bf16[8,256,1024]{2,1,0:T(8,128)(2,1)S(1)}, bf16[8,256,1024]{2,1,0:T(8,128)(2,1)S(1)}, bf16[8,256,128]{2,1,0:T(8,128)(2,1)S(1)}, bf16[8,256,1024]{2,1,0:T(8,128)(2,1)S(1)}, f32[8,4,1024]{2,1,0:T(4,128)S(1)}) custom-call(s32[2]{0:T(128)S(1)} %get-tuple-element.91.refs_0_, ...), custom_call_target="tpu_custom_call", output_to_operand_aliasing={{0}: (7, {}), {1}: (8, {}), {2}: (9, {}), {3}: (10, {}), {4... | custom-call | flops 471859200 | bytes 5242880 | tf_op jit(solution)/shard_map/local/pallas_call | solution.py:320
  128.5 0.0 collective-permute-done.2.refs_2_.refs_3_
  128.5 3.9 %local.11 = (bf16[8,256,1024]{2,1,0:T(8,128)(2,1)S(1)}, bf16[8,256,1024]{2,1,0:T(8,128)(2,1)S(1)}, bf16[8,256,128]{2,1,0:T(8,128)(2,1)S(1)}, bf16[8,256,1024]{2,1,0:T(8,128)(2,1)S(1)}, f32[8,4,1024]{2,1,0:T(4,128)S(1)}) custom-call(s32[2]{0:T(128)S(1)} %get-tuple-element.92.refs_0_, ...), custom_call_target="tpu_custom_call", output_to_operand_aliasing={{0}: (7, {}), {1}: (8, {}), {2}: (9, {}), {3}: (10, {}), {4... | custom-call | flops 471859200 | bytes 5242880 | tf_op jit(solution)/shard_map/local/pallas_call | solution.py:320
  132.4 5.4 %carry.1 = bf16[2048,1024]{1,0:T(8,128)(2,1)} custom-call(bf16[8,256,1024]{2,1,0:T(8,128)(2,1)S(1)} %get-tuple-element.80.refs_0_, bf16[8,256,1024]{2,1,0:T(8,128)(2,1)S(1)} %get-tuple-element.81.refs_1_, bf16[8,256,128]{2,1,0:T(8,128)(2,1)S(1)} %get-tuple-element.82.refs_2_, bf16[8,256,1024]{2,1,0:T(8,128)(2,1)S(1)} %get-tuple-element.83.refs_3_, ...), custom_call_target="tpu_custom_call" | custom-call | flops 629145600 | bytes 16777216 | tf_op jit(solution)/shard_map/carry/pallas_call | solution.py:344
  (3 shorter events, 0.0 us)
Async XLA Ops:
  0.0 16.1 %copy-start = (f32[4,8192]{1,0:T(4,128)S(1)}, f32[4,8192]{1,0:T(4,128)}, u32[]{:S(2)}) copy-start(f32[4,8192]{1,0:T(4,128)} %param.10) | copy-start | bytes 393220
  0.6 65.2 %copy-start.3 = (f32[128]{0:T(128)S(1)}, f32[128]{0:T(128)}, u32[]{:S(2)}) copy-start(f32[128]{0:T(128)} %param.14) | copy-start | bytes 1540
  5.4 32.8 %collective-permute-start.4 = (bf16[264,1280]{1,0:T(8,128)(2,1)}, bf16[264,1280]{1,0:T(8,128)(2,1)S(1)}, u32[]{:S(2)}, u32[]{:S(2)}) collective-permute-start(bf16[264,1280]{1,0:T(8,128)(2,1)} %get-tuple-element.51), channel_id=1, source_target_pairs={{0,4},{1,5},{2,6},{3,7},{4,0},{5,1},{6,2},{7,3},{8,12},{9,13},{10,... | collective-permute-start | bytes 2027528 | tf_op jit(solution)/shard_map/ppermute | solution.py:286
  8.0 58.7 %collective-permute-start.1 = (bf16[264,1280]{1,0:T(8,128)(2,1)}, bf16[264,1280]{1,0:T(8,128)(2,1)}, u32[]{:S(2)}, u32[]{:S(2)}) collective-permute-start(bf16[264,1280]{1,0:T(8,128)(2,1)} %get-tuple-element.47), channel_id=1, source_target_pairs={{0,1},{1,2},{2,3},{3,4},{4,5},{5,6},{6,7},{7,0},{8,9},{9,10},{10,1... | collective-permute-start | bytes 2027528 | tf_op jit(solution)/shard_map/ppermute | solution.py:286
  8.0 74.6 %collective-permute-start.6 = (bf16[264,1280]{1,0:T(8,128)(2,1)}, bf16[264,1280]{1,0:T(8,128)(2,1)S(1)}, u32[]{:S(2)}, u32[]{:S(2)}) collective-permute-start(bf16[264,1280]{1,0:T(8,128)(2,1)} %get-tuple-element.53), channel_id=1, source_target_pairs={{0,3},{1,4},{2,5},{3,6},{4,7},{5,0},{6,1},{7,2},{8,11},{9,12},{10,... | collective-permute-start | bytes 2027528 | tf_op jit(solution)/shard_map/ppermute | solution.py:286
  8.6 76.4 %collective-permute-start.3 = (bf16[264,1280]{1,0:T(8,128)(2,1)}, bf16[264,1280]{1,0:T(8,128)(2,1)S(1)}, u32[]{:S(2)}, u32[]{:S(2)}) collective-permute-start(bf16[264,1280]{1,0:T(8,128)(2,1)} %get-tuple-element.49), channel_id=1, source_target_pairs={{0,7},{1,0},{2,1},{3,2},{4,3},{5,4},{6,5},{7,6},{8,15},{9,8},{10,9... | collective-permute-start | bytes 2027528 | tf_op jit(solution)/shard_map/ppermute | solution.py:286
  9.8 99.9 %collective-permute-start = (bf16[264,1280]{1,0:T(8,128)(2,1)}, bf16[264,1280]{1,0:T(8,128)(2,1)S(1)}, u32[]{:S(2)}, u32[]{:S(2)}) collective-permute-start(bf16[264,1280]{1,0:T(8,128)(2,1)} %get-tuple-element.45), channel_id=1, source_target_pairs={{0,5},{1,6},{2,7},{3,0},{4,1},{5,2},{6,3},{7,4},{8,13},{9,14},{10,... | collective-permute-start | bytes 2027528 | tf_op jit(solution)/shard_map/ppermute | solution.py:286
  38.2 85.9 %collective-permute-start.5 = (bf16[264,1280]{1,0:T(8,128)(2,1)}, bf16[264,1280]{1,0:T(8,128)(2,1)S(1)}, u32[]{:S(2)}, u32[]{:S(2)}) collective-permute-start(bf16[264,1280]{1,0:T(8,128)(2,1)} %get-tuple-element.52), channel_id=1, source_target_pairs={{0,2},{1,3},{2,4},{3,5},{4,6},{5,7},{6,0},{7,1},{8,10},{9,11},{10,... | collective-permute-start | bytes 2027528 | tf_op jit(solution)/shard_map/ppermute | solution.py:286
  66.8 61.8 %collective-permute-start.2 = (bf16[264,1280]{1,0:T(8,128)(2,1)}, bf16[264,1280]{1,0:T(8,128)(2,1)S(1)}, u32[]{:S(2)}, u32[]{:S(2)}) collective-permute-start(bf16[264,1280]{1,0:T(8,128)(2,1)} %get-tuple-element.48), channel_id=1, source_target_pairs={{0,6},{1,7},{2,0},{3,1},{4,2},{5,3},{6,4},{7,5},{8,14},{9,15},{10,... | collective-permute-start | bytes 2027528 | tf_op jit(solution)/shard_map/ppermute | solution.py:286
  69.8 1.1 copy-start.1
  82.6 2.5 %copy-start.2 = (bf16[264,1280]{1,0:T(8,128)(2,1)S(1)}, bf16[264,1280]{1,0:T(8,128)(2,1)}, u32[]{:S(2)}) copy-start(bf16[264,1280]{1,0:T(8,128)(2,1)} %get-tuple-element.54.refs_1_.refs_2_) | copy-start | bytes 2027524

commit v2 on v1

--- a/solution.py
+++ b/solution.py
@@ -22,7 +22,7 @@
 STRIP = 64
 PAIR = 2
 WINDOW = 5
-ORDER = (4, 1, 3, 7, 5, 2, 6)
+ORDER = (1, 7, 4, 2, 6, 3, 5)
 PACK_VMEM = 58 * 1024 * 1024
 VMEM_LIMIT = 28 * 1024 * 1024
 

time: 139 us -> 136 us (0.978)
  starting transfers between devices: 36.1 us -> 14.4 us
  waiting for transfers between devices: 64.8 us -> 83 us
  local copies, waits for them, and re-layouts: 3.47 us -> 5.39 us
  Pallas kernels: 32.8 us -> 31.1 us
    ppermute x7, starting transfers between devices: 36.1 us -> 14.4 us  [per_device(): parts[code] = lax.ppermute(message, 'ctx', pairs)]
    ppermute x7, waiting for transfers between devices: 64.8 us -> 83 us  [per_device(): parts[code] = lax.ppermute(message, 'ctx', pairs)]
    unnamed x8 -> x12, local copies, waits for them, and re-layouts: 1.1 us -> 3.04 us
    pallas_call x6, Pallas kernels: 18.8 us -> 17 us  [per_device(): pl.pallas_call(functools.partial(local_kernel, width, heads, count, bool(...]
  transfers between devices with their start and end apart: 7 -> 7, of which waited for: 4 -> 6; matrix products, arithmetic and copies ran while one was open for 2% -> 2% of each run, Pallas kernels for 14% -> 13%
where the time goes in v2:
time: 136 us; the launch traced here: 135 us
  waiting for transfers between devices  83 us (61%)
  Pallas kernels  31.1 us (23%)
  starting transfers between devices  14.4 us (11%)
  local copies, waits for them, and re-layouts  5.39 us (4%)
    ppermute x7, waiting for transfers between devices, per_device(): parts[code] = lax.ppermute(message, 'ctx', pairs)  83 us
    pallas_call x6, Pallas kernels, per_device(): pl.pallas_call(functools.partial(local_kernel, width, heads, count, bool(...  17 us
    ppermute x7, starting transfers between devices, per_device(): parts[code] = lax.ppermute(message, 'ctx', pairs)  14.4 us
    pallas_call x2, Pallas kernels, pack(): pl.pallas_call(functools.partial(pack_kernel, peers, span, width, heads,...  8.64 us
    pallas_call x1, Pallas kernels, per_device(): pl.pallas_call(functools.partial(carry_kernel, width, whole_group), grid=...  5.45 us
    unnamed x12, local copies, waits for them, and re-layouts  3.04 us
  transfers between devices with their start and end apart: 7, of which 6 were waited for; matrix products, arithmetic and copies ran while one was open for 2% of the time, Pallas kernels for 13%

profile of v2, /device:TPU:12, one launch (start us, length us, event | category | flops | bytes accessed | tf_op | source)
XLA Modules:
  0.0 134.6 jit_solution(4884285044262971794)
XLA Ops:
  0.0 0.0 copy-start
  0.0 0.6 compare_select_fusion.refs_0_
  0.6 0.0 copy-start.5
  0.6 4.8 %pack.2 = (bf16[264,1280]{1,0:T(8,128)(2,1)}, bf16[264,1280]{1,0:T(8,128)(2,1)}, bf16[264,1280]{1,0:T(8,128)(2,1)}, bf16[264,1280]{1,0:T(8,128)(2,1)}, bf16[264,1280]{1,0:T(8,128)(2,1)}) custom-call(s32[8]{0:T(128)} %compare_select_fusion.refs_0_, bf16[256,8192]{1,0:T(8,128)(2,1)} %refs_1_.3, bf16[256,2048]{1,0:T(8,128)(2,1)} %refs_2_.3, ...), custom_call_target="tpu_custom_call" | custom-call | bytes 6553600 | tf_op jit(solution)/shard_map/pack/pallas_call | solution.py:259
  5.4 0.1 collective-permute-start.5
  5.4 1.7 %collective-permute-start.1 = (bf16[264,1280]{1,0:T(8,128)(2,1)}, bf16[264,1280]{1,0:T(8,128)(2,1)S(1)}, u32[]{:S(2)}, u32[]{:S(2)}) collective-permute-start(bf16[264,1280]{1,0:T(8,128)(2,1)} %get-tuple-element.47), channel_id=1, source_target_pairs={{0,7},{1,0},{2,1},{3,2},{4,3},{5,4},{6,5},{7,6},{8,15},{9,8},{10,9... | collective-permute-start | bytes 2027528 | tf_op jit(solution)/shard_map/ppermute | solution.py:286
  7.2 1.6 %collective-permute-start.4 = (bf16[264,1280]{1,0:T(8,128)(2,1)}, bf16[264,1280]{1,0:T(8,128)(2,1)S(1)}, u32[]{:S(2)}, u32[]{:S(2)}) collective-permute-start(bf16[264,1280]{1,0:T(8,128)(2,1)} %get-tuple-element.50), channel_id=1, source_target_pairs={{0,2},{1,3},{2,4},{3,5},{4,6},{5,7},{6,0},{7,1},{8,10},{9,11},{10,... | collective-permute-start | bytes 2027528 | tf_op jit(solution)/shard_map/ppermute | solution.py:286
  8.7 0.7 collective-permute-start.3
  9.4 2.4 %collective-permute-start = (bf16[264,1280]{1,0:T(8,128)(2,1)}, bf16[264,1280]{1,0:T(8,128)(2,1)S(1)}, u32[]{:S(2)}, u32[]{:S(2)}) collective-permute-start(bf16[264,1280]{1,0:T(8,128)(2,1)} %get-tuple-element.45), channel_id=1, source_target_pairs={{0,4},{1,5},{2,6},{3,7},{4,0},{5,1},{6,2},{7,3},{8,12},{9,13},{10,... | collective-permute-start | bytes 2027528 | tf_op jit(solution)/shard_map/ppermute | solution.py:286
  11.8 3.9 %pack.3 = (bf16[264,1280]{1,0:T(8,128)(2,1)}, bf16[264,1280]{1,0:T(8,128)(2,1)}, bf16[264,1280]{1,0:T(8,128)(2,1)}) custom-call(s32[8]{0:T(128)} %compare_select_fusion.refs_0_, bf16[256,8192]{1,0:T(8,128)(2,1)} %refs_1_.3, bf16[256,2048]{1,0:T(8,128)(2,1)} %refs_2_.3, f32[256,128]{1,0:T(8,128)} %refs_3_.3, f32[256,128]{1,0:T(8,128)} %refs_4_.3), custom_call_target="tpu_custom_call" | custom-call | bytes 3932160 | tf_op jit(solution)/shard_map/pack/pallas_call | solution.py:259
  15.7 0.0 copy-done
  15.7 4.8 %collective-permute-done.5.refs_2_.refs_1_ = bf16[264,1280]{1,0:T(8,128)(2,1)S(1)} collective-permute-done((bf16[264,1280]{1,0:T(8,128)(2,1)}, bf16[264,1280]{1,0:T(8,128)(2,1)S(1)}, u32[]{:S(2)}, u32[]{:S(2)}) %collective-permute-start.5) | collective-permute-done | bytes 675872 | tf_op jit(solution)/shard_map/ppermute | solution.py:286
  20.5 0.0 copy-start.1
  20.5 0.8 copy-done.1
  21.3 8.0 %collective-permute-start.6 = (bf16[264,1280]{1,0:T(8,128)(2,1)}, bf16[264,1280]{1,0:T(8,128)(2,1)S(1)}, u32[]{:S(2)}, u32[]{:S(2)}) collective-permute-start(bf16[264,1280]{1,0:T(8,128)(2,1)} %get-tuple-element.53), channel_id=1, source_target_pairs={{0,3},{1,4},{2,5},{3,6},{4,7},{5,0},{6,1},{7,2},{8,11},{9,12},{10,... | collective-permute-start | bytes 2027528 | tf_op jit(solution)/shard_map/ppermute | solution.py:286
  29.3 0.7 fusion.2
  29.9 0.0 copy-done.5
  29.9 0.1 dynamic_slice.18
  30.0 0.1 broadcast_in_dim.4
  30.1 0.1 broadcast_in_dim_reshape.3.refs_4_.refs_6_
  30.2 0.7 dynamic-slice.3
  30.9 13.8 %collective-permute-done.1.refs_1_.refs_2_ = bf16[264,1280]{1,0:T(8,128)(2,1)S(1)} collective-permute-done((bf16[264,1280]{1,0:T(8,128)(2,1)}, bf16[264,1280]{1,0:T(8,128)(2,1)S(1)}, u32[]{:S(2)}, u32[]{:S(2)}) %collective-permute-start.1) | collective-permute-done | bytes 675872 | tf_op jit(solution)/shard_map/ppermute | solution.py:286
  44.6 0.0 collective-permute-start.2
  44.6 0.7 constant_dynamic-slice_fusion.1
  45.3 0.1 fusion.3
  45.4 0.0 copy-start.2
  45.4 1.1 copy-done.2
  46.5 0.0 copy-start.4
  46.5 1.1 copy-done.4
  47.6 2.3 %local.6 = (bf16[8,256,1024]{2,1,0:T(8,128)(2,1)S(1)}, bf16[8,256,1024]{2,1,0:T(8,128)(2,1)S(1)}, bf16[8,256,128]{2,1,0:T(8,128)(2,1)S(1)}, bf16[8,256,1024]{2,1,0:T(8,128)(2,1)S(1)}, f32[8,4,1024]{2,1,0:T(4,128)S(1)}) custom-call(s32[1]{0:T(128)} %get-tuple-element.87.refs_0_, bf16[264,1280]{1,0:T(8,128)(2,1)S(1)} %copy-done.4, ...), custom_call_target="tpu_custom_call" | custom-call | flops 235929600 | bytes 2621440 | tf_op jit(solution)/shard_map/local/pallas_call | solution.py:320
  49.9 0.0 copy-start.3
  49.9 2.4 %local.7 = (bf16[8,256,1024]{2,1,0:T(8,128)(2,1)S(1)}, bf16[8,256,1024]{2,1,0:T(8,128)(2,1)S(1)}, bf16[8,256,128]{2,1,0:T(8,128)(2,1)S(1)}, bf16[8,256,1024]{2,1,0:T(8,128)(2,1)S(1)}, f32[8,4,1024]{2,1,0:T(4,128)S(1)}) custom-call(s32[1]{0:T(128)} %get-tuple-element.88.refs_0_, ...), custom_call_target="tpu_custom_call", output_to_operand_aliasing={{0}: (5, {}), {1}: (6, {}), {2}: (7, {}), {3}: (8, {}), {4}... | custom-call | flops 235929600 | bytes 2621440 | tf_op jit(solution)/shard_map/local/pallas_call | solution.py:320
  52.3 0.0 collective-permute-done.4.refs_2_.refs_1_
  52.3 0.0 copy-done.3
  52.3 2.3 %local.8 = (bf16[8,256,1024]{2,1,0:T(8,128)(2,1)S(1)}, bf16[8,256,1024]{2,1,0:T(8,128)(2,1)S(1)}, bf16[8,256,128]{2,1,0:T(8,128)(2,1)S(1)}, bf16[8,256,1024]{2,1,0:T(8,128)(2,1)S(1)}, f32[8,4,1024]{2,1,0:T(4,128)S(1)}) custom-call(s32[1]{0:T(128)} %get-tuple-element.89.refs_0_, ...), custom_call_target="tpu_custom_call", output_to_operand_aliasing={{0}: (5, {}), {1}: (6, {}), {2}: (7, {}), {3}: (8, {}), {4}... | custom-call | flops 235929600 | bytes 2621440 | tf_op jit(solution)/shard_map/local/pallas_call | solution.py:320
  54.6 39.3 %collective-permute-done.3.refs_1_.refs_4_ = bf16[264,1280]{1,0:T(8,128)(2,1)S(1)} collective-permute-done((bf16[264,1280]{1,0:T(8,128)(2,1)}, bf16[264,1280]{1,0:T(8,128)(2,1)S(1)}, u32[]{:S(2)}, u32[]{:S(2)}) %collective-permute-start.3) | collective-permute-done | bytes 675872 | tf_op jit(solution)/shard_map/ppermute | solution.py:286
  94.0 2.3 %local.9 = (bf16[8,256,1024]{2,1,0:T(8,128)(2,1)S(1)}, bf16[8,256,1024]{2,1,0:T(8,128)(2,1)S(1)}, bf16[8,256,128]{2,1,0:T(8,128)(2,1)S(1)}, bf16[8,256,1024]{2,1,0:T(8,128)(2,1)S(1)}, f32[8,4,1024]{2,1,0:T(4,128)S(1)}) custom-call(s32[1]{0:T(128)} %get-tuple-element.90.refs_0_, ...), custom_call_target="tpu_custom_call", output_to_operand_aliasing={{0}: (5, {}), {1}: (6, {}), {2}: (7, {}), {3}: (8, {}), {4}... | custom-call | flops 235929600 | bytes 2621440 | tf_op jit(solution)/shard_map/local/pallas_call | solution.py:320
  96.2 0.9 collective-permute-done.refs_4_.refs_1_
  97.1 14.5 %collective-permute-done.6.refs_2_.refs_3_ = bf16[264,1280]{1,0:T(8,128)(2,1)S(1)} collective-permute-done((bf16[264,1280]{1,0:T(8,128)(2,1)}, bf16[264,1280]{1,0:T(8,128)(2,1)S(1)}, u32[]{:S(2)}, u32[]{:S(2)}) %collective-permute-start.6) | collective-permute-done | bytes 675872 | tf_op jit(solution)/shard_map/ppermute | solution.py:286
  111.6 3.9 %local.10 = (bf16[8,256,1024]{2,1,0:T(8,128)(2,1)S(1)}, bf16[8,256,1024]{2,1,0:T(8,128)(2,1)S(1)}, bf16[8,256,128]{2,1,0:T(8,128)(2,1)S(1)}, bf16[8,256,1024]{2,1,0:T(8,128)(2,1)S(1)}, f32[8,4,1024]{2,1,0:T(4,128)S(1)}) custom-call(s32[2]{0:T(128)S(1)} %get-tuple-element.91.refs_0_, ...), custom_call_target="tpu_custom_call", output_to_operand_aliasing={{0}: (7, {}), {1}: (8, {}), {2}: (9, {}), {3}: (10, {}), {4... | custom-call | flops 471859200 | bytes 5242880 | tf_op jit(solution)/shard_map/local/pallas_call | solution.py:320
  115.4 9.8 %collective-permute-done.2.refs_2_.refs_3_ = bf16[264,1280]{1,0:T(8,128)(2,1)S(1)} collective-permute-done((bf16[264,1280]{1,0:T(8,128)(2,1)}, bf16[264,1280]{1,0:T(8,128)(2,1)S(1)}, u32[]{:S(2)}, u32[]{:S(2)}) %collective-permute-start.2) | collective-permute-done | bytes 675872 | tf_op jit(solution)/shard_map/ppermute | solution.py:286
  125.3 3.9 %local.11 = (bf16[8,256,1024]{2,1,0:T(8,128)(2,1)S(1)}, bf16[8,256,1024]{2,1,0:T(8,128)(2,1)S(1)}, bf16[8,256,128]{2,1,0:T(8,128)(2,1)S(1)}, bf16[8,256,1024]{2,1,0:T(8,128)(2,1)S(1)}, f32[8,4,1024]{2,1,0:T(4,128)S(1)}) custom-call(s32[2]{0:T(128)S(1)} %get-tuple-element.92.refs_0_, ...), custom_call_target="tpu_custom_call", output_to_operand_aliasing={{0}: (7, {}), {1}: (8, {}), {2}: (9, {}), {3}: (10, {}), {4... | custom-call | flops 471859200 | bytes 5242880 | tf_op jit(solution)/shard_map/local/pallas_call | solution.py:320
  129.1 5.4 %carry.1 = bf16[2048,1024]{1,0:T(8,128)(2,1)} custom-call(bf16[8,256,1024]{2,1,0:T(8,128)(2,1)S(1)} %get-tuple-element.80.refs_0_, bf16[8,256,1024]{2,1,0:T(8,128)(2,1)S(1)} %get-tuple-element.81.refs_1_, bf16[8,256,128]{2,1,0:T(8,128)(2,1)S(1)} %get-tuple-element.82.refs_2_, bf16[8,256,1024]{2,1,0:T(8,128)(2,1)S(1)} %get-tuple-element.83.refs_3_, ...), custom_call_target="tpu_custom_call" | custom-call | flops 629145600 | bytes 16777216 | tf_op jit(solution)/shard_map/carry/pallas_call | solution.py:344
  (3 shorter events, 0.0 us)
Async XLA Ops:
  0.0 15.7 %copy-start = (f32[4,8192]{1,0:T(4,128)S(1)}, f32[4,8192]{1,0:T(4,128)}, u32[]{:S(2)}) copy-start(f32[4,8192]{1,0:T(4,128)} %param.10) | copy-start | bytes 393220
  0.6 29.4 %copy-start.5 = (f32[128]{0:T(128)S(1)}, f32[128]{0:T(128)}, u32[]{:S(2)}) copy-start(f32[128]{0:T(128)} %param.14) | copy-start | bytes 1540
  5.4 15.1 %collective-permute-start.5 = (bf16[264,1280]{1,0:T(8,128)(2,1)}, bf16[264,1280]{1,0:T(8,128)(2,1)S(1)}, u32[]{:S(2)}, u32[]{:S(2)}) collective-permute-start(bf16[264,1280]{1,0:T(8,128)(2,1)} %get-tuple-element.52), channel_id=1, source_target_pairs={{0,1},{1,2},{2,3},{3,4},{4,5},{5,6},{6,7},{7,0},{8,9},{9,10},{10,1... | collective-permute-start | bytes 2027528 | tf_op jit(solution)/shard_map/ppermute | solution.py:286
  5.4 39.2 %collective-permute-start.1 = (bf16[264,1280]{1,0:T(8,128)(2,1)}, bf16[264,1280]{1,0:T(8,128)(2,1)S(1)}, u32[]{:S(2)}, u32[]{:S(2)}) collective-permute-start(bf16[264,1280]{1,0:T(8,128)(2,1)} %get-tuple-element.47), channel_id=1, source_target_pairs={{0,7},{1,0},{2,1},{3,2},{4,3},{5,4},{6,5},{7,6},{8,15},{9,8},{10,9... | collective-permute-start | bytes 2027528 | tf_op jit(solution)/shard_map/ppermute | solution.py:286
  7.2 45.1 %collective-permute-start.4 = (bf16[264,1280]{1,0:T(8,128)(2,1)}, bf16[264,1280]{1,0:T(8,128)(2,1)S(1)}, u32[]{:S(2)}, u32[]{:S(2)}) collective-permute-start(bf16[264,1280]{1,0:T(8,128)(2,1)} %get-tuple-element.50), channel_id=1, source_target_pairs={{0,2},{1,3},{2,4},{3,5},{4,6},{5,7},{6,0},{7,1},{8,10},{9,11},{10,... | collective-permute-start | bytes 2027528 | tf_op jit(solution)/shard_map/ppermute | solution.py:286
  8.7 85.2 %collective-permute-start.3 = (bf16[264,1280]{1,0:T(8,128)(2,1)}, bf16[264,1280]{1,0:T(8,128)(2,1)S(1)}, u32[]{:S(2)}, u32[]{:S(2)}) collective-permute-start(bf16[264,1280]{1,0:T(8,128)(2,1)} %get-tuple-element.49), channel_id=1, source_target_pairs={{0,6},{1,7},{2,0},{3,1},{4,2},{5,3},{6,4},{7,5},{8,14},{9,15},{10,... | collective-permute-start | bytes 2027528 | tf_op jit(solution)/shard_map/ppermute | solution.py:286
  9.4 87.7 %collective-permute-start = (bf16[264,1280]{1,0:T(8,128)(2,1)}, bf16[264,1280]{1,0:T(8,128)(2,1)S(1)}, u32[]{:S(2)}, u32[]{:S(2)}) collective-permute-start(bf16[264,1280]{1,0:T(8,128)(2,1)} %get-tuple-element.45), channel_id=1, source_target_pairs={{0,4},{1,5},{2,6},{3,7},{4,0},{5,1},{6,2},{7,3},{8,12},{9,13},{10,... | collective-permute-start | bytes 2027528 | tf_op jit(solution)/shard_map/ppermute | solution.py:286
  20.5 0.8 copy-start.1
  21.3 90.3 %collective-permute-start.6 = (bf16[264,1280]{1,0:T(8,128)(2,1)}, bf16[264,1280]{1,0:T(8,128)(2,1)S(1)}, u32[]{:S(2)}, u32[]{:S(2)}) collective-permute-start(bf16[264,1280]{1,0:T(8,128)(2,1)} %get-tuple-element.53), channel_id=1, source_target_pairs={{0,3},{1,4},{2,5},{3,6},{4,7},{5,0},{6,1},{7,2},{8,11},{9,12},{10,... | collective-permute-start | bytes 2027528 | tf_op jit(solution)/shard_map/ppermute | solution.py:286
  44.6 80.6 %collective-permute-start.2 = (bf16[264,1280]{1,0:T(8,128)(2,1)}, bf16[264,1280]{1,0:T(8,128)(2,1)S(1)}, u32[]{:S(2)}, u32[]{:S(2)}) collective-permute-start(bf16[264,1280]{1,0:T(8,128)(2,1)} %get-tuple-element.48), channel_id=1, source_target_pairs={{0,5},{1,6},{2,7},{3,0},{4,1},{5,2},{6,3},{7,4},{8,13},{9,14},{10,... | collective-permute-start | bytes 2027528 | tf_op jit(solution)/shard_map/ppermute | solution.py:286
  45.4 1.1 copy-start.2
  46.5 1.1 copy-start.4
  49.9 2.4 %copy-start.3 = (bf16[264,1280]{1,0:T(8,128)(2,1)S(1)}, bf16[264,1280]{1,0:T(8,128)(2,1)}, u32[]{:S(2)}) copy-start(bf16[264,1280]{1,0:T(8,128)(2,1)} %copy-done.1) | copy-start | bytes 2027524

commit v3 on v2

--- a/solution.py
+++ b/solution.py
@@ -23,7 +23,7 @@
 PAIR = 2
 WINDOW = 5
 ORDER = (1, 7, 4, 2, 6, 3, 5)
-PACK_VMEM = 58 * 1024 * 1024
+PACK_VMEM = 50 * 1024 * 1024
 VMEM_LIMIT = 28 * 1024 * 1024
 
 
@@ -52,28 +52,21 @@
 def pack_kernel(peers, span, width, heads, codes, *refs):
     owner_ref, x_ref, kq_ref, decay_ref, step_ref = refs[:5]
     outs = refs[5 : 5 + len(codes)]
-    raw_scalars, scalars, kq_near, sems = refs[5 + len(codes) :]
+    scalars, sems = refs[5 + len(codes) :]
     rows = x_ref.shape[0]
-    copies = [
-        pltpu.make_async_copy(ref, dst, sems.at[1, i])
-        for i, (ref, dst) in enumerate(
-            ((decay_ref, raw_scalars.at[0]), (step_ref, raw_scalars.at[1]), (kq_ref, kq_near))
-        )
-    ]
+    copies = []
     owners = [owner_ref[code] for code in codes]
     for i, owner in enumerate(owners):
         column = pl.multiple_of(owner * width, LANES)
         copies.append(
             pltpu.make_async_copy(
-                x_ref.at[:, pl.ds(column, width)], outs[i].at[0:rows, 0:width], sems.at[0, i]
+                x_ref.at[:, pl.ds(column, width)], outs[i].at[0:rows, 0:width], sems.at[i]
             )
         )
     for copy in copies:
         copy.start()
-    for copy in copies[:3]:
-        copy.wait()
-    for p in range(FIELDS):
-        field = raw_scalars[p].T
+    for p, ref in enumerate((decay_ref, step_ref)):
+        field = ref[...].T
         for owner in range(peers):
             scalars[p, owner] = field[owner * heads : (owner + 1) * heads]
     for i, owner in enumerate(owners):
@@ -85,8 +78,8 @@
         for j in range(2):
             column = pl.multiple_of((j * GROUPS + owner // span) * STATE, LANES)
             left = width + j * STATE
-            outs[i][0:rows, left : left + STATE] = kq_near[:, pl.ds(column, STATE)]
-    for copy in copies[3:]:
+            outs[i][0:rows, left : left + STATE] = kq_ref[:, pl.ds(column, STATE)]
+    for copy in copies:
         copy.wait()
 
 
@@ -258,14 +251,12 @@
         shape = jax.ShapeDtypeStruct((rows + scalar_rows, full), jnp.bfloat16)
         return pl.pallas_call(
             functools.partial(pack_kernel, peers, span, width, heads, codes),
-            in_specs=[smem] + [hbm] * 4,
+            in_specs=[smem, hbm] + [vmem] * 3,
             out_specs=[vmem] * len(codes),
             out_shape=[shape] * len(codes),
             scratch_shapes=[
-                pltpu.VMEM((FIELDS, rows, HEADS), jnp.float32),
                 pltpu.VMEM((FIELDS, peers, heads, rows), jnp.float32),
-                pltpu.VMEM(key_query.shape, jnp.bfloat16),
-                pltpu.SemaphoreType.DMA((2, max(3, len(codes)))),
+                pltpu.SemaphoreType.DMA((len(codes),)),
             ],
             compiler_params=pltpu.CompilerParams(vmem_limit_bytes=PACK_VMEM),
             cost_estimate=pl.CostEstimate(

time: 136 us -> 138 us (1.015)
  waiting for transfers between devices: 83 us -> 79.9 us
  Pallas kernels: 31.1 us -> 33.8 us
  local copies, waits for them, and re-layouts: 5.39 us -> 7.92 us
    pallas_call x6, Pallas kernels: 17 us -> 21.6 us  [per_device(): pl.pallas_call(functools.partial(local_kernel, width, heads, count, bool(...]
    ppermute x7, waiting for transfers between devices: 83 us -> 79.9 us  [per_device(): parts[code] = lax.ppermute(message, 'ctx', pairs)]
    unnamed x12 -> x22, local copies, waits for them, and re-layouts: 3.04 us -> 5.55 us
    pallas_call x2, Pallas kernels: 8.64 us -> 6.79 us  [pack(): pl.pallas_call(functools.partial(pack_kernel, peers, span, width, heads,...]
  transfers between devices with their start and end apart: 7 -> 7, of which waited for: 6 -> 5; matrix products, arithmetic and copies ran while one was open for 2% -> 2% of each run, Pallas kernels for 13% -> 14%
where the time goes in v3:
time: 138 us; the launch traced here: 136 us
  waiting for transfers between devices  79.9 us (58%)
  Pallas kernels  33.8 us (24%)
  starting transfers between devices  14.3 us (10%)
  local copies, waits for them, and re-layouts  7.92 us (6%)
    ppermute x7, waiting for transfers between devices, per_device(): parts[code] = lax.ppermute(message, 'ctx', pairs)  79.9 us
    pallas_call x6, Pallas kernels, per_device(): pl.pallas_call(functools.partial(local_kernel, width, heads, count, bool(...  21.6 us
    ppermute x7, starting transfers between devices, per_device(): parts[code] = lax.ppermute(message, 'ctx', pairs)  14.3 us
    pallas_call x2, Pallas kernels, pack(): pl.pallas_call(functools.partial(pack_kernel, peers, span, width, heads,...  6.79 us
    unnamed x22, local copies, waits for them, and re-layouts  5.55 us
    pallas_call x1, Pallas kernels, per_device(): pl.pallas_call(functools.partial(carry_kernel, width, whole_group), grid=...  5.48 us
  transfers between devices with their start and end apart: 7, of which 5 were waited for; matrix products, arithmetic and copies ran while one was open for 2% of the time, Pallas kernels for 14%

profile of v3, /device:TPU:12, one launch (start us, length us, event | category | flops | bytes accessed | tf_op | source)
XLA Modules:
  0.0 136.0 jit_solution(2688057903252125556)
XLA Ops:
  0.0 0.0 copy-start
  0.0 0.0 copy-start.1
  0.0 0.0 copy-start.4
  0.0 1.0 copy-done.4
  1.0 0.0 copy-start.6
  1.0 0.9 copy-done.6
  1.9 0.0 copy-start.5
  1.9 0.0 copy-start.7
  1.9 0.0 copy-start.10
  1.9 4.8 %pack.2 = (bf16[264,1280]{1,0:T(8,128)(2,1)}, bf16[264,1280]{1,0:T(8,128)(2,1)}, bf16[264,1280]{1,0:T(8,128)(2,1)}, bf16[264,1280]{1,0:T(8,128)(2,1)}, bf16[264,1280]{1,0:T(8,128)(2,1)}) custom-call(s32[8]{0:T(128)S(1)} %compare_select_fusion.refs_0_, bf16[256,8192]{1,0:T(8,128)(2,1)} %refs_1_.3, bf16[256,2048]{1,0:T(8,128)(2,1)} %refs_2_.3, ...), custom_call_target="tpu_custom_call" | custom-call | bytes 6553600 | tf_op jit(solution)/shard_map/pack/pallas_call | solution.py:252
  6.8 0.1 collective-permute-start.5
  6.8 1.7 %collective-permute-start.1 = (bf16[264,1280]{1,0:T(8,128)(2,1)}, bf16[264,1280]{1,0:T(8,128)(2,1)}, u32[]{:S(2)}, u32[]{:S(2)}) collective-permute-start(bf16[264,1280]{1,0:T(8,128)(2,1)} %get-tuple-element.47), channel_id=1, source_target_pairs={{0,7},{1,0},{2,1},{3,2},{4,3},{5,4},{6,5},{7,6},{8,15},{9,8},{10,9... | collective-permute-start | bytes 2027528 | tf_op jit(solution)/shard_map/ppermute | solution.py:277
  8.6 1.6 %collective-permute-start.4 = (bf16[264,1280]{1,0:T(8,128)(2,1)}, bf16[264,1280]{1,0:T(8,128)(2,1)S(1)}, u32[]{:S(2)}, u32[]{:S(2)}) collective-permute-start(bf16[264,1280]{1,0:T(8,128)(2,1)} %get-tuple-element.50), channel_id=1, source_target_pairs={{0,2},{1,3},{2,4},{3,5},{4,6},{5,7},{6,0},{7,1},{8,10},{9,11},{10,... | collective-permute-start | bytes 2027528 | tf_op jit(solution)/shard_map/ppermute | solution.py:277
  10.1 0.7 collective-permute-start.3
  10.8 2.4 %collective-permute-start = (bf16[264,1280]{1,0:T(8,128)(2,1)}, bf16[264,1280]{1,0:T(8,128)(2,1)S(1)}, u32[]{:S(2)}, u32[]{:S(2)}) collective-permute-start(bf16[264,1280]{1,0:T(8,128)(2,1)} %get-tuple-element.45), channel_id=1, source_target_pairs={{0,4},{1,5},{2,6},{3,7},{4,0},{5,1},{6,2},{7,3},{8,12},{9,13},{10,... | collective-permute-start | bytes 2027528 | tf_op jit(solution)/shard_map/ppermute | solution.py:277
  13.2 0.0 copy-done.1
  13.2 0.0 copy-done.5
  13.2 0.0 copy-done.7
  13.2 2.0 %pack.3 = (bf16[264,1280]{1,0:T(8,128)(2,1)S(1)}, bf16[264,1280]{1,0:T(8,128)(2,1)S(1)}, bf16[264,1280]{1,0:T(8,128)(2,1)S(1)}) custom-call(s32[8]{0:T(128)S(1)} %compare_select_fusion.refs_0_, bf16[256,8192]{1,0:T(8,128)(2,1)} %refs_1_.3, bf16[256,2048]{1,0:T(8,128)(2,1)S(1)} %copy-done.1, f32[256,128]{1,0:T(8,128)S(1)} %copy-done.5, f32[256,128]{1,0:T(8,128)S(1)} %copy-done.7), custom_call_target="tpu_custom_call" | custom-call | bytes 3932160 | tf_op jit(solution)/shard_map/pack/pallas_call | solution.py:252
  15.2 0.0 copy-start.2
  15.2 0.8 copy-done.2
  16.0 0.0 copy-start.8
  16.0 0.8 copy-done.8
  16.9 0.0 copy-start.9
  16.9 0.9 copy-done.9
  17.7 0.0 copy-done
  17.7 4.3 %collective-permute-done.5.refs_2_.refs_1_ = bf16[264,1280]{1,0:T(8,128)(2,1)} collective-permute-done((bf16[264,1280]{1,0:T(8,128)(2,1)}, bf16[264,1280]{1,0:T(8,128)(2,1)}, u32[]{:S(2)}, u32[]{:S(2)}) %collective-permute-start.5) | collective-permute-done | bytes 675872 | tf_op jit(solution)/shard_map/ppermute | solution.py:277
  22.0 7.9 %collective-permute-start.6 = (bf16[264,1280]{1,0:T(8,128)(2,1)}, bf16[264,1280]{1,0:T(8,128)(2,1)S(1)}, u32[]{:S(2)}, u32[]{:S(2)}) collective-permute-start(bf16[264,1280]{1,0:T(8,128)(2,1)} %copy-done.9), channel_id=1, source_target_pairs={{0,3},{1,4},{2,5},{3,6},{4,7},{5,0},{6,1},{7,2},{8,11},{9,12},{10,... | collective-permute-start | bytes 2027528 | tf_op jit(solution)/shard_map/ppermute | solution.py:277
  29.8 0.7 fusion.2
  30.5 0.0 copy-done.10
  30.5 0.1 dynamic_slice.18
  30.6 0.1 broadcast_in_dim.4
  30.7 0.1 broadcast_in_dim_reshape.3.refs_4_.refs_6_
  30.7 0.7 dynamic-slice.3
  31.4 14.6 %collective-permute-done.1.refs_1_.refs_2_ = bf16[264,1280]{1,0:T(8,128)(2,1)} collective-permute-done((bf16[264,1280]{1,0:T(8,128)(2,1)}, bf16[264,1280]{1,0:T(8,128)(2,1)}, u32[]{:S(2)}, u32[]{:S(2)}) %collective-permute-start.1) | collective-permute-done | bytes 675872 | tf_op jit(solution)/shard_map/ppermute | solution.py:277
  46.0 0.0 collective-permute-start.2
  46.0 0.7 constant_dynamic-slice_fusion.1
  46.7 0.1 fusion.3
  46.8 0.0 copy-start.3
  46.8 1.1 copy-done.3
  47.9 3.5 %local.6 = (bf16[8,256,1024]{2,1,0:T(8,128)(2,1)S(1)}, bf16[8,256,1024]{2,1,0:T(8,128)(2,1)S(1)}, bf16[8,256,128]{2,1,0:T(8,128)(2,1)S(1)}, bf16[8,256,1024]{2,1,0:T(8,128)(2,1)S(1)}, f32[8,4,1024]{2,1,0:T(4,128)S(1)}) custom-call(s32[1]{0:T(128)} %get-tuple-element.87.refs_0_, bf16[264,1280]{1,0:T(8,128)(2,1)S(1)} %copy-done.3, ...), custom_call_target="tpu_custom_call" | custom-call | flops 235929600 | bytes 2621440 | tf_op jit(solution)/shard_map/local/pallas_call | solution.py:311
  51.4 3.4 %local.7 = (bf16[8,256,1024]{2,1,0:T(8,128)(2,1)S(1)}, bf16[8,256,1024]{2,1,0:T(8,128)(2,1)S(1)}, bf16[8,256,128]{2,1,0:T(8,128)(2,1)S(1)}, bf16[8,256,1024]{2,1,0:T(8,128)(2,1)S(1)}, f32[8,4,1024]{2,1,0:T(4,128)S(1)}) custom-call(s32[1]{0:T(128)} %get-tuple-element.88.refs_0_, ...), custom_call_target="tpu_custom_call", output_to_operand_aliasing={{0}: (5, {}), {1}: (6, {}), {2}: (7, {}), {3}: (8, {}), {4}... | custom-call | flops 235929600 | bytes 2621440 | tf_op jit(solution)/shard_map/local/pallas_call | solution.py:311
  54.8 0.0 collective-permute-done.4.refs_2_.refs_1_
  54.8 3.5 %local.8 = (bf16[8,256,1024]{2,1,0:T(8,128)(2,1)S(1)}, bf16[8,256,1024]{2,1,0:T(8,128)(2,1)S(1)}, bf16[8,256,128]{2,1,0:T(8,128)(2,1)S(1)}, bf16[8,256,1024]{2,1,0:T(8,128)(2,1)S(1)}, f32[8,4,1024]{2,1,0:T(4,128)S(1)}) custom-call(s32[1]{0:T(128)} %get-tuple-element.89.refs_0_, ...), custom_call_target="tpu_custom_call", output_to_operand_aliasing={{0}: (5, {}), {1}: (6, {}), {2}: (7, {}), {3}: (8, {}), {4}... | custom-call | flops 235929600 | bytes 2621440 | tf_op jit(solution)/shard_map/local/pallas_call | solution.py:311
  58.3 37.1 %collective-permute-done.3.refs_1_.refs_4_ = bf16[264,1280]{1,0:T(8,128)(2,1)S(1)} collective-permute-done((bf16[264,1280]{1,0:T(8,128)(2,1)}, bf16[264,1280]{1,0:T(8,128)(2,1)S(1)}, u32[]{:S(2)}, u32[]{:S(2)}) %collective-permute-start.3) | collective-permute-done | bytes 675872 | tf_op jit(solution)/shard_map/ppermute | solution.py:277
  95.3 3.5 %local.9 = (bf16[8,256,1024]{2,1,0:T(8,128)(2,1)S(1)}, bf16[8,256,1024]{2,1,0:T(8,128)(2,1)S(1)}, bf16[8,256,128]{2,1,0:T(8,128)(2,1)S(1)}, bf16[8,256,1024]{2,1,0:T(8,128)(2,1)S(1)}, f32[8,4,1024]{2,1,0:T(4,128)S(1)}) custom-call(s32[1]{0:T(128)} %get-tuple-element.90.refs_0_, ...), custom_call_target="tpu_custom_call", output_to_operand_aliasing={{0}: (5, {}), {1}: (6, {}), {2}: (7, {}), {3}: (8, {}), {4}... | custom-call | flops 235929600 | bytes 2621440 | tf_op jit(solution)/shard_map/local/pallas_call | solution.py:311
  98.8 0.0 collective-permute-done.refs_4_.refs_1_
  98.8 14.2 %collective-permute-done.6.refs_2_.refs_3_ = bf16[264,1280]{1,0:T(8,128)(2,1)S(1)} collective-permute-done((bf16[264,1280]{1,0:T(8,128)(2,1)}, bf16[264,1280]{1,0:T(8,128)(2,1)S(1)}, u32[]{:S(2)}, u32[]{:S(2)}) %collective-permute-start.6) | collective-permute-done | bytes 675872 | tf_op jit(solution)/shard_map/ppermute | solution.py:277
  113.0 3.9 %local.10 = (bf16[8,256,1024]{2,1,0:T(8,128)(2,1)S(1)}, bf16[8,256,1024]{2,1,0:T(8,128)(2,1)S(1)}, bf16[8,256,128]{2,1,0:T(8,128)(2,1)S(1)}, bf16[8,256,1024]{2,1,0:T(8,128)(2,1)S(1)}, f32[8,4,1024]{2,1,0:T(4,128)S(1)}) custom-call(s32[2]{0:T(128)S(1)} %get-tuple-element.91.refs_0_, ...), custom_call_target="tpu_custom_call", output_to_operand_aliasing={{0}: (7, {}), {1}: (8, {}), {2}: (9, {}), {3}: (10, {}), {4... | custom-call | flops 471859200 | bytes 5242880 | tf_op jit(solution)/shard_map/local/pallas_call | solution.py:311
  116.9 9.8 %collective-permute-done.2.refs_2_.refs_3_ = bf16[264,1280]{1,0:T(8,128)(2,1)S(1)} collective-permute-done((bf16[264,1280]{1,0:T(8,128)(2,1)}, bf16[264,1280]{1,0:T(8,128)(2,1)S(1)}, u32[]{:S(2)}, u32[]{:S(2)}) %collective-permute-start.2) | collective-permute-done | bytes 675872 | tf_op jit(solution)/shard_map/ppermute | solution.py:277
  126.7 3.9 %local.11 = (bf16[8,256,1024]{2,1,0:T(8,128)(2,1)S(1)}, bf16[8,256,1024]{2,1,0:T(8,128)(2,1)S(1)}, bf16[8,256,128]{2,1,0:T(8,128)(2,1)S(1)}, bf16[8,256,1024]{2,1,0:T(8,128)(2,1)S(1)}, f32[8,4,1024]{2,1,0:T(4,128)S(1)}) custom-call(s32[2]{0:T(128)S(1)} %get-tuple-element.92.refs_0_, ...), custom_call_target="tpu_custom_call", output_to_operand_aliasing={{0}: (7, {}), {1}: (8, {}), {2}: (9, {}), {3}: (10, {}), {4... | custom-call | flops 471859200 | bytes 5242880 | tf_op jit(solution)/shard_map/local/pallas_call | solution.py:311
  130.6 5.5 %carry.1 = bf16[2048,1024]{1,0:T(8,128)(2,1)} custom-call(bf16[8,256,1024]{2,1,0:T(8,128)(2,1)S(1)} %get-tuple-element.80.refs_0_, bf16[8,256,1024]{2,1,0:T(8,128)(2,1)S(1)} %get-tuple-element.81.refs_1_, bf16[8,256,128]{2,1,0:T(8,128)(2,1)S(1)} %get-tuple-element.82.refs_2_, bf16[8,256,1024]{2,1,0:T(8,128)(2,1)S(1)} %get-tuple-element.83.refs_3_, ...), custom_call_target="tpu_custom_call" | custom-call | flops 629145600 | bytes 16777216 | tf_op jit(solution)/shard_map/carry/pallas_call | solution.py:335
  (4 shorter events, 0.0 us)
Async XLA Ops:
  0.0 17.7 %copy-start = (f32[4,8192]{1,0:T(4,128)S(1)}, f32[4,8192]{1,0:T(4,128)}, u32[]{:S(2)}) copy-start(f32[4,8192]{1,0:T(4,128)} %param.10) | copy-start | bytes 393220
  0.0 13.2 %copy-start.1 = (bf16[256,2048]{1,0:T(8,128)(2,1)S(1)}, bf16[256,2048]{1,0:T(8,128)(2,1)}, u32[]{:S(2)}) copy-start(bf16[256,2048]{1,0:T(8,128)(2,1)} %refs_2_.3) | copy-start | bytes 3145732
  0.0 1.0 copy-start.4
  1.0 0.9 copy-start.6
  1.9 11.3 %copy-start.5 = (f32[256,128]{1,0:T(8,128)S(1)}, f32[256,128]{1,0:T(8,128)}, u32[]{:S(2)}) copy-start(f32[256,128]{1,0:T(8,128)} %refs_3_.3) | copy-start | bytes 393220
  1.9 11.3 %copy-start.7 = (f32[256,128]{1,0:T(8,128)S(1)}, f32[256,128]{1,0:T(8,128)}, u32[]{:S(2)}) copy-start(f32[256,128]{1,0:T(8,128)} %refs_4_.3) | copy-start | bytes 393220
  1.9 28.6 %copy-start.10 = (f32[128]{0:T(128)S(1)}, f32[128]{0:T(128)}, u32[]{:S(2)}) copy-start(f32[128]{0:T(128)} %param.14) | copy-start | bytes 1540
  6.8 15.2 %collective-permute-start.5 = (bf16[264,1280]{1,0:T(8,128)(2,1)}, bf16[264,1280]{1,0:T(8,128)(2,1)}, u32[]{:S(2)}, u32[]{:S(2)}) collective-permute-start(bf16[264,1280]{1,0:T(8,128)(2,1)} %get-tuple-element.52), channel_id=1, source_target_pairs={{0,1},{1,2},{2,3},{3,4},{4,5},{5,6},{6,7},{7,0},{8,9},{9,10},{10,1... | collective-permute-start | bytes 2027528 | tf_op jit(solution)/shard_map/ppermute | solution.py:277
  6.8 39.2 %collective-permute-start.1 = (bf16[264,1280]{1,0:T(8,128)(2,1)}, bf16[264,1280]{1,0:T(8,128)(2,1)}, u32[]{:S(2)}, u32[]{:S(2)}) collective-permute-start(bf16[264,1280]{1,0:T(8,128)(2,1)} %get-tuple-element.47), channel_id=1, source_target_pairs={{0,7},{1,0},{2,1},{3,2},{4,3},{5,4},{6,5},{7,6},{8,15},{9,8},{10,9... | collective-permute-start | bytes 2027528 | tf_op jit(solution)/shard_map/ppermute | solution.py:277
  8.6 46.2 %collective-permute-start.4 = (bf16[264,1280]{1,0:T(8,128)(2,1)}, bf16[264,1280]{1,0:T(8,128)(2,1)S(1)}, u32[]{:S(2)}, u32[]{:S(2)}) collective-permute-start(bf16[264,1280]{1,0:T(8,128)(2,1)} %get-tuple-element.50), channel_id=1, source_target_pairs={{0,2},{1,3},{2,4},{3,5},{4,6},{5,7},{6,0},{7,1},{8,10},{9,11},{10,... | collective-permute-start | bytes 2027528 | tf_op jit(solution)/shard_map/ppermute | solution.py:277
  10.1 85.2 %collective-permute-start.3 = (bf16[264,1280]{1,0:T(8,128)(2,1)}, bf16[264,1280]{1,0:T(8,128)(2,1)S(1)}, u32[]{:S(2)}, u32[]{:S(2)}) collective-permute-start(bf16[264,1280]{1,0:T(8,128)(2,1)} %get-tuple-element.49), channel_id=1, source_target_pairs={{0,6},{1,7},{2,0},{3,1},{4,2},{5,3},{6,4},{7,5},{8,14},{9,15},{10,... | collective-permute-start | bytes 2027528 | tf_op jit(solution)/shard_map/ppermute | solution.py:277
  10.8 88.0 %collective-permute-start = (bf16[264,1280]{1,0:T(8,128)(2,1)}, bf16[264,1280]{1,0:T(8,128)(2,1)S(1)}, u32[]{:S(2)}, u32[]{:S(2)}) collective-permute-start(bf16[264,1280]{1,0:T(8,128)(2,1)} %get-tuple-element.45), channel_id=1, source_target_pairs={{0,4},{1,5},{2,6},{3,7},{4,0},{5,1},{6,2},{7,3},{8,12},{9,13},{10,... | collective-permute-start | bytes 2027528 | tf_op jit(solution)/shard_map/ppermute | solution.py:277
  15.2 0.9 copy-start.2
  16.0 0.8 copy-start.8
  16.9 0.9 copy-start.9
  22.0 91.0 %collective-permute-start.6 = (bf16[264,1280]{1,0:T(8,128)(2,1)}, bf16[264,1280]{1,0:T(8,128)(2,1)S(1)}, u32[]{:S(2)}, u32[]{:S(2)}) collective-permute-start(bf16[264,1280]{1,0:T(8,128)(2,1)} %copy-done.9), channel_id=1, source_target_pairs={{0,3},{1,4},{2,5},{3,6},{4,7},{5,0},{6,1},{7,2},{8,11},{9,12},{10,... | collective-permute-start | bytes 2027528 | tf_op jit(solution)/shard_map/ppermute | solution.py:277
  46.0 80.6 %collective-permute-start.2 = (bf16[264,1280]{1,0:T(8,128)(2,1)}, bf16[264,1280]{1,0:T(8,128)(2,1)S(1)}, u32[]{:S(2)}, u32[]{:S(2)}) collective-permute-start(bf16[264,1280]{1,0:T(8,128)(2,1)} %copy-done.8), channel_id=1, source_target_pairs={{0,5},{1,6},{2,7},{3,0},{4,1},{5,2},{6,3},{7,4},{8,13},{9,14},{10,... | collective-permute-start | bytes 2027528 | tf_op jit(solution)/shard_map/ppermute | solution.py:277
  46.8 1.1 copy-start.3

commit v4 on v2

--- a/solution.py
+++ b/solution.py
@@ -276,8 +276,8 @@
 
     codes = [code for code in ORDER if code < peers]
     codes += [code for code in range(1, peers) if code not in codes]
-    parts = dict(zip(codes[:WINDOW], pack(codes[:WINDOW])))
-    parts.update(zip(codes[WINDOW:] + [0], pack(codes[WINDOW:] + [0])))
+    parts = dict(zip(codes[:2], pack(codes[:2])))
+    parts.update(zip(codes[2:] + [0], pack(codes[2:] + [0])))
     for i, code in enumerate(codes):
         pairs = [(j, (j + code) % peers) for j in range(peers)]
         message = parts[code]

time: 136 us -> 134 us (0.985)
  starting transfers between devices: 14.4 us -> 11.2 us
  waiting for transfers between devices: 83 us -> 85 us
    ppermute x7, starting transfers between devices: 14.4 us -> 11.2 us  [per_device(): parts[code] = lax.ppermute(message, 'ctx', pairs)]
    ppermute x7, waiting for transfers between devices: 83 us -> 85 us  [per_device(): parts[code] = lax.ppermute(message, 'ctx', pairs)]
  transfers between devices with their start and end apart: 7 -> 7, of which waited for: 6 -> 6; matrix products, arithmetic and copies ran while one was open for 2% -> 2% of each run, Pallas kernels for 13% -> 14%
where the time goes in v4:
time: 134 us; the launch traced here: 133 us
  waiting for transfers between devices  85 us (63%)
  Pallas kernels  31.1 us (23%)
  starting transfers between devices  11.2 us (8%)
  local copies, waits for them, and re-layouts  5.4 us (4%)
    ppermute x7, waiting for transfers between devices, per_device(): parts[code] = lax.ppermute(message, 'ctx', pairs)  85 us
    pallas_call x6, Pallas kernels, per_device(): pl.pallas_call(functools.partial(local_kernel, width, heads, count, bool(...  17 us
    ppermute x7, starting transfers between devices, per_device(): parts[code] = lax.ppermute(message, 'ctx', pairs)  11.2 us
    pallas_call x2, Pallas kernels, pack(): pl.pallas_call(functools.partial(pack_kernel, peers, span, width, heads,...  8.65 us
    pallas_call x1, Pallas kernels, per_device(): pl.pallas_call(functools.partial(carry_kernel, width, whole_group), grid=...  5.45 us
    unnamed x12, local copies, waits for them, and re-layouts  3.05 us
  transfers between devices with their start and end apart: 7, of which 6 were waited for; matrix products, arithmetic and copies ran while one was open for 2% of the time, Pallas kernels for 14%

profile of v4, /device:TPU:12, one launch (start us, length us, event | category | flops | bytes accessed | tf_op | source)
XLA Modules:
  0.0 133.4 jit_solution(8927605759889078957)
XLA Ops:
  0.0 0.0 copy-start
  0.0 0.6 compare_select_fusion.refs_0_
  0.6 0.0 copy-start.5
  0.6 3.6 %pack.3 = (bf16[264,1280]{1,0:T(8,128)(2,1)}, bf16[264,1280]{1,0:T(8,128)(2,1)}) custom-call(s32[8]{0:T(128)} %compare_select_fusion.refs_0_, bf16[256,8192]{1,0:T(8,128)(2,1)} %refs_1_.3, bf16[256,2048]{1,0:T(8,128)(2,1)} %refs_2_.3, f32[256,128]{1,0:T(8,128)} %refs_3_.3, f32[256,128]{1,0:T(8,128)} %refs_4_.3), custom_call_target="tpu_custom_call" | custom-call | bytes 2621440 | tf_op jit(solution)/shard_map/pack/pallas_call | solution.py:259
  4.2 0.1 collective-permute-start.5
  4.3 1.7 %collective-permute-start.1 = (bf16[264,1280]{1,0:T(8,128)(2,1)}, bf16[264,1280]{1,0:T(8,128)(2,1)S(1)}, u32[]{:S(2)}, u32[]{:S(2)}) collective-permute-start(bf16[264,1280]{1,0:T(8,128)(2,1)} %get-tuple-element.47), channel_id=1, source_target_pairs={{0,7},{1,0},{2,1},{3,2},{4,3},{5,4},{6,5},{7,6},{8,15},{9,8},{10,9... | collective-permute-start | bytes 2027528 | tf_op jit(solution)/shard_map/ppermute | solution.py:286
  6.0 5.0 %pack.2 = (bf16[264,1280]{1,0:T(8,128)(2,1)}, bf16[264,1280]{1,0:T(8,128)(2,1)}, bf16[264,1280]{1,0:T(8,128)(2,1)}, bf16[264,1280]{1,0:T(8,128)(2,1)}, bf16[264,...) custom-call(s32[8]{0:T(128)} %compare_select_fusion.refs_0_, bf16[256,8192]{1,0:T(8,128)(2,1)} %refs_1_.3, ...), custom_call_target="tpu_custom_call" | custom-call | bytes 7864320 | tf_op jit(solution)/shard_map/pack/pallas_call | solution.py:259
  11.0 1.6 %collective-permute-start.4 = (bf16[264,1280]{1,0:T(8,128)(2,1)}, bf16[264,1280]{1,0:T(8,128)(2,1)S(1)}, u32[]{:S(2)}, u32[]{:S(2)}) collective-permute-start(bf16[264,1280]{1,0:T(8,128)(2,1)} %get-tuple-element.50), channel_id=1, source_target_pairs={{0,2},{1,3},{2,4},{3,5},{4,6},{5,7},{6,0},{7,1},{8,10},{9,11},{10,... | collective-permute-start | bytes 2027528 | tf_op jit(solution)/shard_map/ppermute | solution.py:286
  12.7 0.7 collective-permute-start.3
  13.4 2.3 %collective-permute-start = (bf16[264,1280]{1,0:T(8,128)(2,1)}, bf16[264,1280]{1,0:T(8,128)(2,1)S(1)}, u32[]{:S(2)}, u32[]{:S(2)}) collective-permute-start(bf16[264,1280]{1,0:T(8,128)(2,1)} %get-tuple-element.45), channel_id=1, source_target_pairs={{0,4},{1,5},{2,6},{3,7},{4,0},{5,1},{6,2},{7,3},{8,12},{9,13},{10,... | collective-permute-start | bytes 2027528 | tf_op jit(solution)/shard_map/ppermute | solution.py:286
  15.7 0.0 copy-done
  15.7 3.6 %collective-permute-done.5.refs_2_.refs_1_ = bf16[264,1280]{1,0:T(8,128)(2,1)S(1)} collective-permute-done((bf16[264,1280]{1,0:T(8,128)(2,1)}, bf16[264,1280]{1,0:T(8,128)(2,1)S(1)}, u32[]{:S(2)}, u32[]{:S(2)}) %collective-permute-start.5) | collective-permute-done | bytes 675872 | tf_op jit(solution)/shard_map/ppermute | solution.py:286
  19.3 0.0 copy-start.1
  19.3 0.9 copy-done.1
  20.2 4.8 %collective-permute-start.6 = (bf16[264,1280]{1,0:T(8,128)(2,1)}, bf16[264,1280]{1,0:T(8,128)(2,1)S(1)}, u32[]{:S(2)}, u32[]{:S(2)}) collective-permute-start(bf16[264,1280]{1,0:T(8,128)(2,1)} %get-tuple-element.53), channel_id=1, source_target_pairs={{0,3},{1,4},{2,5},{3,6},{4,7},{5,0},{6,1},{7,2},{8,11},{9,12},{10,... | collective-permute-start | bytes 2027528 | tf_op jit(solution)/shard_map/ppermute | solution.py:286
  24.9 0.7 fusion.2
  25.6 0.0 copy-done.5
  25.6 0.1 dynamic_slice.18
  25.7 0.1 broadcast_in_dim.4
  25.7 0.1 broadcast_in_dim_reshape.3.refs_4_.refs_6_
  25.8 0.7 dynamic-slice.3
  26.5 15.1 %collective-permute-done.1.refs_1_.refs_2_ = bf16[264,1280]{1,0:T(8,128)(2,1)S(1)} collective-permute-done((bf16[264,1280]{1,0:T(8,128)(2,1)}, bf16[264,1280]{1,0:T(8,128)(2,1)S(1)}, u32[]{:S(2)}, u32[]{:S(2)}) %collective-permute-start.1) | collective-permute-done | bytes 675872 | tf_op jit(solution)/shard_map/ppermute | solution.py:286
  41.6 0.0 collective-permute-start.2
  41.6 0.7 constant_dynamic-slice_fusion.1
  42.3 0.1 fusion.3
  42.4 0.0 copy-start.2
  42.4 1.1 copy-done.2
  43.5 0.0 copy-start.4
  43.5 1.1 copy-done.4
  44.6 2.3 %local.6 = (bf16[8,256,1024]{2,1,0:T(8,128)(2,1)S(1)}, bf16[8,256,1024]{2,1,0:T(8,128)(2,1)S(1)}, bf16[8,256,128]{2,1,0:T(8,128)(2,1)S(1)}, bf16[8,256,1024]{2,1,0:T(8,128)(2,1)S(1)}, f32[8,4,1024]{2,1,0:T(4,128)S(1)}) custom-call(s32[1]{0:T(128)} %get-tuple-element.87.refs_0_, bf16[264,1280]{1,0:T(8,128)(2,1)S(1)} %copy-done.4, ...), custom_call_target="tpu_custom_call" | custom-call | flops 235929600 | bytes 2621440 | tf_op jit(solution)/shard_map/local/pallas_call | solution.py:320
  46.9 0.0 copy-start.3
  46.9 2.4 %local.7 = (bf16[8,256,1024]{2,1,0:T(8,128)(2,1)S(1)}, bf16[8,256,1024]{2,1,0:T(8,128)(2,1)S(1)}, bf16[8,256,128]{2,1,0:T(8,128)(2,1)S(1)}, bf16[8,256,1024]{2,1,0:T(8,128)(2,1)S(1)}, f32[8,4,1024]{2,1,0:T(4,128)S(1)}) custom-call(s32[1]{0:T(128)} %get-tuple-element.88.refs_0_, ...), custom_call_target="tpu_custom_call", output_to_operand_aliasing={{0}: (5, {}), {1}: (6, {}), {2}: (7, {}), {3}: (8, {}), {4}... | custom-call | flops 235929600 | bytes 2621440 | tf_op jit(solution)/shard_map/local/pallas_call | solution.py:320
  49.3 0.0 collective-permute-done.4.refs_2_.refs_1_
  49.3 0.0 copy-done.3
  49.3 2.3 %local.8 = (bf16[8,256,1024]{2,1,0:T(8,128)(2,1)S(1)}, bf16[8,256,1024]{2,1,0:T(8,128)(2,1)S(1)}, bf16[8,256,128]{2,1,0:T(8,128)(2,1)S(1)}, bf16[8,256,1024]{2,1,0:T(8,128)(2,1)S(1)}, f32[8,4,1024]{2,1,0:T(4,128)S(1)}) custom-call(s32[1]{0:T(128)} %get-tuple-element.89.refs_0_, ...), custom_call_target="tpu_custom_call", output_to_operand_aliasing={{0}: (5, {}), {1}: (6, {}), {2}: (7, {}), {3}: (8, {}), {4}... | custom-call | flops 235929600 | bytes 2621440 | tf_op jit(solution)/shard_map/local/pallas_call | solution.py:320
  51.6 36.4 %collective-permute-done.3.refs_1_.refs_4_ = bf16[264,1280]{1,0:T(8,128)(2,1)S(1)} collective-permute-done((bf16[264,1280]{1,0:T(8,128)(2,1)}, bf16[264,1280]{1,0:T(8,128)(2,1)S(1)}, u32[]{:S(2)}, u32[]{:S(2)}) %collective-permute-start.3) | collective-permute-done | bytes 675872 | tf_op jit(solution)/shard_map/ppermute | solution.py:286
  88.0 2.3 %local.9 = (bf16[8,256,1024]{2,1,0:T(8,128)(2,1)S(1)}, bf16[8,256,1024]{2,1,0:T(8,128)(2,1)S(1)}, bf16[8,256,128]{2,1,0:T(8,128)(2,1)S(1)}, bf16[8,256,1024]{2,1,0:T(8,128)(2,1)S(1)}, f32[8,4,1024]{2,1,0:T(4,128)S(1)}) custom-call(s32[1]{0:T(128)} %get-tuple-element.90.refs_0_, ...), custom_call_target="tpu_custom_call", output_to_operand_aliasing={{0}: (5, {}), {1}: (6, {}), {2}: (7, {}), {3}: (8, {}), {4}... | custom-call | flops 235929600 | bytes 2621440 | tf_op jit(solution)/shard_map/local/pallas_call | solution.py:320
  90.3 8.2 %collective-permute-done.refs_4_.refs_1_ = bf16[264,1280]{1,0:T(8,128)(2,1)S(1)} collective-permute-done((bf16[264,1280]{1,0:T(8,128)(2,1)}, bf16[264,1280]{1,0:T(8,128)(2,1)S(1)}, u32[]{:S(2)}, u32[]{:S(2)}) %collective-permute-start) | collective-permute-done | bytes 675872 | tf_op jit(solution)/shard_map/ppermute | solution.py:286
  98.6 14.5 %collective-permute-done.6.refs_2_.refs_3_ = bf16[264,1280]{1,0:T(8,128)(2,1)S(1)} collective-permute-done((bf16[264,1280]{1,0:T(8,128)(2,1)}, bf16[264,1280]{1,0:T(8,128)(2,1)S(1)}, u32[]{:S(2)}, u32[]{:S(2)}) %collective-permute-start.6) | collective-permute-done | bytes 675872 | tf_op jit(solution)/shard_map/ppermute | solution.py:286
  113.1 3.9 %local.10 = (bf16[8,256,1024]{2,1,0:T(8,128)(2,1)S(1)}, bf16[8,256,1024]{2,1,0:T(8,128)(2,1)S(1)}, bf16[8,256,128]{2,1,0:T(8,128)(2,1)S(1)}, bf16[8,256,1024]{2,1,0:T(8,128)(2,1)S(1)}, f32[8,4,1024]{2,1,0:T(4,128)S(1)}) custom-call(s32[2]{0:T(128)S(1)} %get-tuple-element.91.refs_0_, ...), custom_call_target="tpu_custom_call", output_to_operand_aliasing={{0}: (7, {}), {1}: (8, {}), {2}: (9, {}), {3}: (10, {}), {4... | custom-call | flops 471859200 | bytes 5242880 | tf_op jit(solution)/shard_map/local/pallas_call | solution.py:320
  116.9 7.2 %collective-permute-done.2.refs_2_.refs_3_ = bf16[264,1280]{1,0:T(8,128)(2,1)S(1)} collective-permute-done((bf16[264,1280]{1,0:T(8,128)(2,1)}, bf16[264,1280]{1,0:T(8,128)(2,1)S(1)}, u32[]{:S(2)}, u32[]{:S(2)}) %collective-permute-start.2) | collective-permute-done | bytes 675872 | tf_op jit(solution)/shard_map/ppermute | solution.py:286
  124.1 3.9 %local.11 = (bf16[8,256,1024]{2,1,0:T(8,128)(2,1)S(1)}, bf16[8,256,1024]{2,1,0:T(8,128)(2,1)S(1)}, bf16[8,256,128]{2,1,0:T(8,128)(2,1)S(1)}, bf16[8,256,1024]{2,1,0:T(8,128)(2,1)S(1)}, f32[8,4,1024]{2,1,0:T(4,128)S(1)}) custom-call(s32[2]{0:T(128)S(1)} %get-tuple-element.92.refs_0_, ...), custom_call_target="tpu_custom_call", output_to_operand_aliasing={{0}: (7, {}), {1}: (8, {}), {2}: (9, {}), {3}: (10, {}), {4... | custom-call | flops 471859200 | bytes 5242880 | tf_op jit(solution)/shard_map/local/pallas_call | solution.py:320
  128.0 5.4 %carry.1 = bf16[2048,1024]{1,0:T(8,128)(2,1)} custom-call(bf16[8,256,1024]{2,1,0:T(8,128)(2,1)S(1)} %get-tuple-element.80.refs_0_, bf16[8,256,1024]{2,1,0:T(8,128)(2,1)S(1)} %get-tuple-element.81.refs_1_, bf16[8,256,128]{2,1,0:T(8,128)(2,1)S(1)} %get-tuple-element.82.refs_2_, bf16[8,256,1024]{2,1,0:T(8,128)(2,1)S(1)} %get-tuple-element.83.refs_3_, ...), custom_call_target="tpu_custom_call" | custom-call | flops 629145600 | bytes 16777216 | tf_op jit(solution)/shard_map/carry/pallas_call | solution.py:344
  (3 shorter events, 0.0 us)
Async XLA Ops:
  0.0 15.7 %copy-start = (f32[4,8192]{1,0:T(4,128)S(1)}, f32[4,8192]{1,0:T(4,128)}, u32[]{:S(2)}) copy-start(f32[4,8192]{1,0:T(4,128)} %param.10) | copy-start | bytes 393220
  0.6 25.0 %copy-start.5 = (f32[128]{0:T(128)S(1)}, f32[128]{0:T(128)}, u32[]{:S(2)}) copy-start(f32[128]{0:T(128)} %param.14) | copy-start | bytes 1540
  4.2 15.1 %collective-permute-start.5 = (bf16[264,1280]{1,0:T(8,128)(2,1)}, bf16[264,1280]{1,0:T(8,128)(2,1)S(1)}, u32[]{:S(2)}, u32[]{:S(2)}) collective-permute-start(bf16[264,1280]{1,0:T(8,128)(2,1)} %get-tuple-element.52), channel_id=1, source_target_pairs={{0,1},{1,2},{2,3},{3,4},{4,5},{5,6},{6,7},{7,0},{8,9},{9,10},{10,1... | collective-permute-start | bytes 2027528 | tf_op jit(solution)/shard_map/ppermute | solution.py:286
  4.3 37.3 %collective-permute-start.1 = (bf16[264,1280]{1,0:T(8,128)(2,1)}, bf16[264,1280]{1,0:T(8,128)(2,1)S(1)}, u32[]{:S(2)}, u32[]{:S(2)}) collective-permute-start(bf16[264,1280]{1,0:T(8,128)(2,1)} %get-tuple-element.47), channel_id=1, source_target_pairs={{0,7},{1,0},{2,1},{3,2},{4,3},{5,4},{6,5},{7,6},{8,15},{9,8},{10,9... | collective-permute-start | bytes 2027528 | tf_op jit(solution)/shard_map/ppermute | solution.py:286
  11.0 38.2 %collective-permute-start.4 = (bf16[264,1280]{1,0:T(8,128)(2,1)}, bf16[264,1280]{1,0:T(8,128)(2,1)S(1)}, u32[]{:S(2)}, u32[]{:S(2)}) collective-permute-start(bf16[264,1280]{1,0:T(8,128)(2,1)} %get-tuple-element.50), channel_id=1, source_target_pairs={{0,2},{1,3},{2,4},{3,5},{4,6},{5,7},{6,0},{7,1},{8,10},{9,11},{10,... | collective-permute-start | bytes 2027528 | tf_op jit(solution)/shard_map/ppermute | solution.py:286
  12.7 75.3 %collective-permute-start.3 = (bf16[264,1280]{1,0:T(8,128)(2,1)}, bf16[264,1280]{1,0:T(8,128)(2,1)S(1)}, u32[]{:S(2)}, u32[]{:S(2)}) collective-permute-start(bf16[264,1280]{1,0:T(8,128)(2,1)} %get-tuple-element.49), channel_id=1, source_target_pairs={{0,6},{1,7},{2,0},{3,1},{4,2},{5,3},{6,4},{7,5},{8,14},{9,15},{10,... | collective-permute-start | bytes 2027528 | tf_op jit(solution)/shard_map/ppermute | solution.py:286
  13.4 85.2 %collective-permute-start = (bf16[264,1280]{1,0:T(8,128)(2,1)}, bf16[264,1280]{1,0:T(8,128)(2,1)S(1)}, u32[]{:S(2)}, u32[]{:S(2)}) collective-permute-start(bf16[264,1280]{1,0:T(8,128)(2,1)} %get-tuple-element.45), channel_id=1, source_target_pairs={{0,4},{1,5},{2,6},{3,7},{4,0},{5,1},{6,2},{7,3},{8,12},{9,13},{10,... | collective-permute-start | bytes 2027528 | tf_op jit(solution)/shard_map/ppermute | solution.py:286
  19.3 0.9 copy-start.1
  20.2 92.9 %collective-permute-start.6 = (bf16[264,1280]{1,0:T(8,128)(2,1)}, bf16[264,1280]{1,0:T(8,128)(2,1)S(1)}, u32[]{:S(2)}, u32[]{:S(2)}) collective-permute-start(bf16[264,1280]{1,0:T(8,128)(2,1)} %get-tuple-element.53), channel_id=1, source_target_pairs={{0,3},{1,4},{2,5},{3,6},{4,7},{5,0},{6,1},{7,2},{8,11},{9,12},{10,... | collective-permute-start | bytes 2027528 | tf_op jit(solution)/shard_map/ppermute | solution.py:286
  41.6 82.5 %collective-permute-start.2 = (bf16[264,1280]{1,0:T(8,128)(2,1)}, bf16[264,1280]{1,0:T(8,128)(2,1)S(1)}, u32[]{:S(2)}, u32[]{:S(2)}) collective-permute-start(bf16[264,1280]{1,0:T(8,128)(2,1)} %get-tuple-element.48), channel_id=1, source_target_pairs={{0,5},{1,6},{2,7},{3,0},{4,1},{5,2},{6,3},{7,4},{8,13},{9,14},{10,... | collective-permute-start | bytes 2027528 | tf_op jit(solution)/shard_map/ppermute | solution.py:286
  42.4 1.1 copy-start.2
  43.5 1.1 copy-start.4
  46.9 2.4 %copy-start.3 = (bf16[264,1280]{1,0:T(8,128)(2,1)S(1)}, bf16[264,1280]{1,0:T(8,128)(2,1)}, u32[]{:S(2)}) copy-start(bf16[264,1280]{1,0:T(8,128)(2,1)} %copy-done.1) | copy-start | bytes 2027524

commit v5 on v4

--- a/solution.py
+++ b/solution.py
@@ -22,7 +22,7 @@
 STRIP = 64
 PAIR = 2
 WINDOW = 5
-ORDER = (1, 7, 4, 2, 6, 3, 5)
+ORDER = (1, 7, 4, 2, 6, 5, 3)
 PACK_VMEM = 58 * 1024 * 1024
 VMEM_LIMIT = 28 * 1024 * 1024
 

time: 134 us -> 137 us (1.022)
  the two profiles are of different devices: /device:TPU:12 before, /device:TPU:1 now
where the time goes in v5:
time: 137 us; the launch traced here: 136 us
  waiting for transfers between devices  83.6 us (61%)
  Pallas kernels  31.1 us (23%)
  starting transfers between devices  15.6 us (11%)
  local copies, waits for them, and re-layouts  5.4 us (4%)
    ppermute x7, waiting for transfers between devices, per_device(): parts[code] = lax.ppermute(message, 'ctx', pairs)  83.6 us
    pallas_call x6, Pallas kernels, per_device(): pl.pallas_call(functools.partial(local_kernel, width, heads, count, bool(...  17 us
    ppermute x7, starting transfers between devices, per_device(): parts[code] = lax.ppermute(message, 'ctx', pairs)  15.6 us
    pallas_call x2, Pallas kernels, pack(): pl.pallas_call(functools.partial(pack_kernel, peers, span, width, heads,...  8.65 us
    pallas_call x1, Pallas kernels, per_device(): pl.pallas_call(functools.partial(carry_kernel, width, whole_group), grid=...  5.45 us
    unnamed x12, local copies, waits for them, and re-layouts  3.05 us
  transfers between devices with their start and end apart: 7, of which 4 were waited for; matrix products, arithmetic and copies ran while one was open for 2% of the time, Pallas kernels for 13%

profile of v5, /device:TPU:1, one launch (start us, length us, event | category | flops | bytes accessed | tf_op | source)
XLA Modules:
  0.0 136.5 jit_solution(9970348235589857576)
XLA Ops:
  0.0 0.0 copy-start
  0.0 0.6 compare_select_fusion.refs_0_
  0.6 0.0 copy-start.5
  0.6 3.6 %pack.3 = (bf16[264,1280]{1,0:T(8,128)(2,1)}, bf16[264,1280]{1,0:T(8,128)(2,1)}) custom-call(s32[8]{0:T(128)} %compare_select_fusion.refs_0_, bf16[256,8192]{1,0:T(8,128)(2,1)} %refs_1_.3, bf16[256,2048]{1,0:T(8,128)(2,1)} %refs_2_.3, f32[256,128]{1,0:T(8,128)} %refs_3_.3, f32[256,128]{1,0:T(8,128)} %refs_4_.3), custom_call_target="tpu_custom_call" | custom-call | bytes 2621440 | tf_op jit(solution)/shard_map/pack/pallas_call | solution.py:259
  4.2 2.7 %collective-permute-start.4 = (bf16[264,1280]{1,0:T(8,128)(2,1)}, bf16[264,1280]{1,0:T(8,128)(2,1)S(1)}, u32[]{:S(2)}, u32[]{:S(2)}) collective-permute-start(bf16[264,1280]{1,0:T(8,128)(2,1)} %get-tuple-element.51), channel_id=1, source_target_pairs={{0,1},{1,2},{2,3},{3,4},{4,5},{5,6},{6,7},{7,0},{8,9},{9,10},{10,1... | collective-permute-start | bytes 2027528 | tf_op jit(solution)/shard_map/ppermute | solution.py:286
  6.9 0.0 collective-permute-start.1
  6.9 5.0 %pack.2 = (bf16[264,1280]{1,0:T(8,128)(2,1)}, bf16[264,1280]{1,0:T(8,128)(2,1)}, bf16[264,1280]{1,0:T(8,128)(2,1)}, bf16[264,1280]{1,0:T(8,128)(2,1)}, bf16[264,...) custom-call(s32[8]{0:T(128)} %compare_select_fusion.refs_0_, bf16[256,8192]{1,0:T(8,128)(2,1)} %refs_1_.3, ...), custom_call_target="tpu_custom_call" | custom-call | bytes 7864320 | tf_op jit(solution)/shard_map/pack/pallas_call | solution.py:259
  12.0 1.3 collective-permute-start
  13.3 2.0 %collective-permute-start.6 = (bf16[264,1280]{1,0:T(8,128)(2,1)}, bf16[264,1280]{1,0:T(8,128)(2,1)S(1)}, u32[]{:S(2)}, u32[]{:S(2)}) collective-permute-start(bf16[264,1280]{1,0:T(8,128)(2,1)} %get-tuple-element.53), channel_id=1, source_target_pairs={{0,6},{1,7},{2,0},{3,1},{4,2},{5,3},{6,4},{7,5},{8,14},{9,15},{10,... | collective-permute-start | bytes 2027528 | tf_op jit(solution)/shard_map/ppermute | solution.py:286
  15.3 0.5 collective-permute-start.3
  15.8 0.0 copy-done
  15.8 4.2 %collective-permute-done.4.refs_2_.refs_1_ = bf16[264,1280]{1,0:T(8,128)(2,1)S(1)} collective-permute-done((bf16[264,1280]{1,0:T(8,128)(2,1)}, bf16[264,1280]{1,0:T(8,128)(2,1)S(1)}, u32[]{:S(2)}, u32[]{:S(2)}) %collective-permute-start.4) | collective-permute-done | bytes 675872 | tf_op jit(solution)/shard_map/ppermute | solution.py:286
  20.1 0.0 copy-start.1
  20.1 0.9 copy-done.1
  20.9 9.1 %collective-permute-start.5 = (bf16[264,1280]{1,0:T(8,128)(2,1)}, bf16[264,1280]{1,0:T(8,128)(2,1)S(1)}, u32[]{:S(2)}, u32[]{:S(2)}) collective-permute-start(bf16[264,1280]{1,0:T(8,128)(2,1)} %get-tuple-element.52), channel_id=1, source_target_pairs={{0,5},{1,6},{2,7},{3,0},{4,1},{5,2},{6,3},{7,4},{8,13},{9,14},{10,... | collective-permute-start | bytes 2027528 | tf_op jit(solution)/shard_map/ppermute | solution.py:286
  30.0 0.7 fusion.2
  30.6 0.0 copy-done.5
  30.6 0.1 dynamic_slice.18
  30.7 0.1 broadcast_in_dim.4
  30.8 0.1 broadcast_in_dim_reshape.3.refs_4_.refs_6_
  30.9 0.7 dynamic-slice.3
  31.6 12.3 %collective-permute-done.1.refs_1_.refs_2_ = bf16[264,1280]{1,0:T(8,128)(2,1)S(1)} collective-permute-done((bf16[264,1280]{1,0:T(8,128)(2,1)}, bf16[264,1280]{1,0:T(8,128)(2,1)S(1)}, u32[]{:S(2)}, u32[]{:S(2)}) %collective-permute-start.1) | collective-permute-done | bytes 675872 | tf_op jit(solution)/shard_map/ppermute | solution.py:286
  43.8 0.0 collective-permute-start.2
  43.8 0.7 constant_dynamic-slice_fusion.1
  44.5 0.1 fusion.3
  44.6 0.0 copy-start.2
  44.6 1.1 copy-done.2
  45.7 0.0 copy-start.4
  45.7 1.1 copy-done.4
  46.8 2.3 %local.6 = (bf16[8,256,1024]{2,1,0:T(8,128)(2,1)S(1)}, bf16[8,256,1024]{2,1,0:T(8,128)(2,1)S(1)}, bf16[8,256,128]{2,1,0:T(8,128)(2,1)S(1)}, bf16[8,256,1024]{2,1,0:T(8,128)(2,1)S(1)}, f32[8,4,1024]{2,1,0:T(4,128)S(1)}) custom-call(s32[1]{0:T(128)} %get-tuple-element.87.refs_0_, bf16[264,1280]{1,0:T(8,128)(2,1)S(1)} %copy-done.4, ...), custom_call_target="tpu_custom_call" | custom-call | flops 235929600 | bytes 2621440 | tf_op jit(solution)/shard_map/local/pallas_call | solution.py:320
  49.1 0.0 copy-start.3
  49.1 2.4 %local.7 = (bf16[8,256,1024]{2,1,0:T(8,128)(2,1)S(1)}, bf16[8,256,1024]{2,1,0:T(8,128)(2,1)S(1)}, bf16[8,256,128]{2,1,0:T(8,128)(2,1)S(1)}, bf16[8,256,1024]{2,1,0:T(8,128)(2,1)S(1)}, f32[8,4,1024]{2,1,0:T(4,128)S(1)}) custom-call(s32[1]{0:T(128)} %get-tuple-element.88.refs_0_, ...), custom_call_target="tpu_custom_call", output_to_operand_aliasing={{0}: (5, {}), {1}: (6, {}), {2}: (7, {}), {3}: (8, {}), {4}... | custom-call | flops 235929600 | bytes 2621440 | tf_op jit(solution)/shard_map/local/pallas_call | solution.py:320
  51.5 0.0 collective-permute-done.refs_2_.refs_1_
  51.5 0.0 copy-done.3
  51.5 2.3 %local.8 = (bf16[8,256,1024]{2,1,0:T(8,128)(2,1)S(1)}, bf16[8,256,1024]{2,1,0:T(8,128)(2,1)S(1)}, bf16[8,256,128]{2,1,0:T(8,128)(2,1)S(1)}, bf16[8,256,1024]{2,1,0:T(8,128)(2,1)S(1)}, f32[8,4,1024]{2,1,0:T(4,128)S(1)}) custom-call(s32[1]{0:T(128)} %get-tuple-element.89.refs_0_, ...), custom_call_target="tpu_custom_call", output_to_operand_aliasing={{0}: (5, {}), {1}: (6, {}), {2}: (7, {}), {3}: (8, {}), {4}... | custom-call | flops 235929600 | bytes 2621440 | tf_op jit(solution)/shard_map/local/pallas_call | solution.py:320
  53.8 0.0 collective-permute-done.6.refs_1_.refs_4_
  53.8 2.3 %local.9 = (bf16[8,256,1024]{2,1,0:T(8,128)(2,1)S(1)}, bf16[8,256,1024]{2,1,0:T(8,128)(2,1)S(1)}, bf16[8,256,128]{2,1,0:T(8,128)(2,1)S(1)}, bf16[8,256,1024]{2,1,0:T(8,128)(2,1)S(1)}, f32[8,4,1024]{2,1,0:T(4,128)S(1)}) custom-call(s32[1]{0:T(128)} %get-tuple-element.90.refs_0_, ...), custom_call_target="tpu_custom_call", output_to_operand_aliasing={{0}: (5, {}), {1}: (6, {}), {2}: (7, {}), {3}: (8, {}), {4}... | custom-call | flops 235929600 | bytes 2621440 | tf_op jit(solution)/shard_map/local/pallas_call | solution.py:320
  56.2 43.0 %collective-permute-done.3.refs_1_.refs_4_ = bf16[264,1280]{1,0:T(8,128)(2,1)S(1)} collective-permute-done((bf16[264,1280]{1,0:T(8,128)(2,1)}, bf16[264,1280]{1,0:T(8,128)(2,1)S(1)}, u32[]{:S(2)}, u32[]{:S(2)}) %collective-permute-start.3) | collective-permute-done | bytes 675872 | tf_op jit(solution)/shard_map/ppermute | solution.py:286
  99.2 24.1 %collective-permute-done.5.refs_2_.refs_3_ = bf16[264,1280]{1,0:T(8,128)(2,1)S(1)} collective-permute-done((bf16[264,1280]{1,0:T(8,128)(2,1)}, bf16[264,1280]{1,0:T(8,128)(2,1)S(1)}, u32[]{:S(2)}, u32[]{:S(2)}) %collective-permute-start.5) | collective-permute-done | bytes 675872 | tf_op jit(solution)/shard_map/ppermute | solution.py:286
  123.3 3.9 %local.10 = (bf16[8,256,1024]{2,1,0:T(8,128)(2,1)S(1)}, bf16[8,256,1024]{2,1,0:T(8,128)(2,1)S(1)}, bf16[8,256,128]{2,1,0:T(8,128)(2,1)S(1)}, bf16[8,256,1024]{2,1,0:T(8,128)(2,1)S(1)}, f32[8,4,1024]{2,1,0:T(4,128)S(1)}) custom-call(s32[2]{0:T(128)S(1)} %get-tuple-element.91.refs_0_, ...), custom_call_target="tpu_custom_call", output_to_operand_aliasing={{0}: (7, {}), {1}: (8, {}), {2}: (9, {}), {3}: (10, {}), {4... | custom-call | flops 471859200 | bytes 5242880 | tf_op jit(solution)/shard_map/local/pallas_call | solution.py:320
  127.1 0.0 collective-permute-done.2.refs_2_.refs_3_
  127.1 3.9 %local.11 = (bf16[8,256,1024]{2,1,0:T(8,128)(2,1)S(1)}, bf16[8,256,1024]{2,1,0:T(8,128)(2,1)S(1)}, bf16[8,256,128]{2,1,0:T(8,128)(2,1)S(1)}, bf16[8,256,1024]{2,1,0:T(8,128)(2,1)S(1)}, f32[8,4,1024]{2,1,0:T(4,128)S(1)}) custom-call(s32[2]{0:T(128)S(1)} %get-tuple-element.92.refs_0_, ...), custom_call_target="tpu_custom_call", output_to_operand_aliasing={{0}: (7, {}), {1}: (8, {}), {2}: (9, {}), {3}: (10, {}), {4... | custom-call | flops 471859200 | bytes 5242880 | tf_op jit(solution)/shard_map/local/pallas_call | solution.py:320
  131.0 5.4 %carry.1 = bf16[2048,1024]{1,0:T(8,128)(2,1)} custom-call(bf16[8,256,1024]{2,1,0:T(8,128)(2,1)S(1)} %get-tuple-element.80.refs_0_, bf16[8,256,1024]{2,1,0:T(8,128)(2,1)S(1)} %get-tuple-element.81.refs_1_, bf16[8,256,128]{2,1,0:T(8,128)(2,1)S(1)} %get-tuple-element.82.refs_2_, bf16[8,256,1024]{2,1,0:T(8,128)(2,1)S(1)} %get-tuple-element.83.refs_3_, ...), custom_call_target="tpu_custom_call" | custom-call | flops 629145600 | bytes 16777216 | tf_op jit(solution)/shard_map/carry/pallas_call | solution.py:344
  (3 shorter events, 0.0 us)
Async XLA Ops:
  0.0 15.8 %copy-start = (f32[4,8192]{1,0:T(4,128)S(1)}, f32[4,8192]{1,0:T(4,128)}, u32[]{:S(2)}) copy-start(f32[4,8192]{1,0:T(4,128)} %param.10) | copy-start | bytes 393220
  0.6 30.1 %copy-start.5 = (f32[128]{0:T(128)S(1)}, f32[128]{0:T(128)}, u32[]{:S(2)}) copy-start(f32[128]{0:T(128)} %param.14) | copy-start | bytes 1540
  4.2 15.9 %collective-permute-start.4 = (bf16[264,1280]{1,0:T(8,128)(2,1)}, bf16[264,1280]{1,0:T(8,128)(2,1)S(1)}, u32[]{:S(2)}, u32[]{:S(2)}) collective-permute-start(bf16[264,1280]{1,0:T(8,128)(2,1)} %get-tuple-element.51), channel_id=1, source_target_pairs={{0,1},{1,2},{2,3},{3,4},{4,5},{5,6},{6,7},{7,0},{8,9},{9,10},{10,1... | collective-permute-start | bytes 2027528 | tf_op jit(solution)/shard_map/ppermute | solution.py:286
  6.9 36.9 %collective-permute-start.1 = (bf16[264,1280]{1,0:T(8,128)(2,1)}, bf16[264,1280]{1,0:T(8,128)(2,1)S(1)}, u32[]{:S(2)}, u32[]{:S(2)}) collective-permute-start(bf16[264,1280]{1,0:T(8,128)(2,1)} %get-tuple-element.47), channel_id=1, source_target_pairs={{0,7},{1,0},{2,1},{3,2},{4,3},{5,4},{6,5},{7,6},{8,15},{9,8},{10,9... | collective-permute-start | bytes 2027528 | tf_op jit(solution)/shard_map/ppermute | solution.py:286
  12.0 39.5 %collective-permute-start = (bf16[264,1280]{1,0:T(8,128)(2,1)}, bf16[264,1280]{1,0:T(8,128)(2,1)S(1)}, u32[]{:S(2)}, u32[]{:S(2)}) collective-permute-start(bf16[264,1280]{1,0:T(8,128)(2,1)} %get-tuple-element.45), channel_id=1, source_target_pairs={{0,2},{1,3},{2,4},{3,5},{4,6},{5,7},{6,0},{7,1},{8,10},{9,11},{10,... | collective-permute-start | bytes 2027528 | tf_op jit(solution)/shard_map/ppermute | solution.py:286
  13.3 40.5 %collective-permute-start.6 = (bf16[264,1280]{1,0:T(8,128)(2,1)}, bf16[264,1280]{1,0:T(8,128)(2,1)S(1)}, u32[]{:S(2)}, u32[]{:S(2)}) collective-permute-start(bf16[264,1280]{1,0:T(8,128)(2,1)} %get-tuple-element.53), channel_id=1, source_target_pairs={{0,6},{1,7},{2,0},{3,1},{4,2},{5,3},{6,4},{7,5},{8,14},{9,15},{10,... | collective-permute-start | bytes 2027528 | tf_op jit(solution)/shard_map/ppermute | solution.py:286
  15.3 83.9 %collective-permute-start.3 = (bf16[264,1280]{1,0:T(8,128)(2,1)}, bf16[264,1280]{1,0:T(8,128)(2,1)S(1)}, u32[]{:S(2)}, u32[]{:S(2)}) collective-permute-start(bf16[264,1280]{1,0:T(8,128)(2,1)} %get-tuple-element.49), channel_id=1, source_target_pairs={{0,4},{1,5},{2,6},{3,7},{4,0},{5,1},{6,2},{7,3},{8,12},{9,13},{10,... | collective-permute-start | bytes 2027528 | tf_op jit(solution)/shard_map/ppermute | solution.py:286
  20.1 0.9 copy-start.1
  20.9 102.4 %collective-permute-start.5 = (bf16[264,1280]{1,0:T(8,128)(2,1)}, bf16[264,1280]{1,0:T(8,128)(2,1)S(1)}, u32[]{:S(2)}, u32[]{:S(2)}) collective-permute-start(bf16[264,1280]{1,0:T(8,128)(2,1)} %get-tuple-element.52), channel_id=1, source_target_pairs={{0,5},{1,6},{2,7},{3,0},{4,1},{5,2},{6,3},{7,4},{8,13},{9,14},{10,... | collective-permute-start | bytes 2027528 | tf_op jit(solution)/shard_map/ppermute | solution.py:286
  43.8 83.3 %collective-permute-start.2 = (bf16[264,1280]{1,0:T(8,128)(2,1)}, bf16[264,1280]{1,0:T(8,128)(2,1)S(1)}, u32[]{:S(2)}, u32[]{:S(2)}) collective-permute-start(bf16[264,1280]{1,0:T(8,128)(2,1)} %get-tuple-element.48), channel_id=1, source_target_pairs={{0,3},{1,4},{2,5},{3,6},{4,7},{5,0},{6,1},{7,2},{8,11},{9,12},{10,... | collective-permute-start | bytes 2027528 | tf_op jit(solution)/shard_map/ppermute | solution.py:286
  44.6 1.1 copy-start.2
  45.7 1.1 copy-start.4
  49.1 2.4 %copy-start.3 = (bf16[264,1280]{1,0:T(8,128)(2,1)S(1)}, bf16[264,1280]{1,0:T(8,128)(2,1)}, u32[]{:S(2)}) copy-start(bf16[264,1280]{1,0:T(8,128)(2,1)} %copy-done.1) | copy-start | bytes 2027524
